TPU v7x, 32 devices: a whole 2x2x4 slice. The times are simulated.
32 devices in a mesh: expert: 16 (over z, x, core), shard: 2 (over y).
Axes of the slice: x: 2, y: 2, z: 4, core: 2. Of those that a mesh axis runs over, the one named last changes fastest.
Arguments:
- hidden_in: bfloat16 [4096, 1024], P(('expert', 'shard')), may hold values from -6 to 6
- norm_attn: bfloat16 [1024], P('shard'), may hold values from 0.5 to 1.5
- w_query: bfloat16 [1024, 1024], P('shard'), may hold values from -0.75 to 0.75
- w_key: bfloat16 [1024, 512], P('shard'), may hold values from -0.75 to 0.75
- w_value: bfloat16 [1024, 512], P('shard'), may hold values from -0.1875 to 0.1875
- w_out: bfloat16 [1024, 1024], P('shard'), may hold values from -2.5 to 2.5
- norm_ffn: bfloat16 [1024], P('shard'), may hold values from 0.5 to 1.5
- w_router: bfloat16 [1024, 16], P('shard'), may hold values from -0.09375 to 0.09375
- w_gate_up: bfloat16 [16, 1024, 1024], P('expert'), may hold values from -0.1875 to 0.1875
- w_down: bfloat16 [16, 512, 1024], P('expert'), may hold values from -3 to 3
- routes: int32 [4096, 8], P(('expert', 'shard')), may hold values from 0 to 15, all different within a row; in each aligned block of 128 rows (0 to 127, 128 to 255, ...) at most 80 rows name the same one
- out_grad: bfloat16 [4096, 1024], P(('expert', 'shard')), may hold values from -6 to 6
Outputs:
- output: bfloat16 [4096, 1024], P(('expert', 'shard'))
- input_grad: bfloat16 [4096, 1024], P(('expert', 'shard'))
- norm_attn_grad: float32 [1024], P('shard')
- query_wgrad: float32 [1024, 1024], P('shard')
- key_wgrad: float32 [1024, 512], P('shard')
- value_wgrad: float32 [1024, 512], P('shard')
- out_wgrad: float32 [1024, 1024], P('shard')
- norm_ffn_grad: float32 [1024], P('shard')
- router_wgrad: float32 [1024, 16], P('shard')
- gate_up_wgrad: float32 [16, 1024, 1024], P('expert', None, 'shard')
- down_wgrad: float32 [16, 512, 1024], P('expert', None, 'shard')
Inputs may be any that keep to these rules, and one draw needn't show every extreme that they name: `routes`: among the 128 rows of one device (aligned blocks), no expert is named by more than 80 rows, and in some block one expert is named by exactly 80; a row names 8 different experts.
All inputs are finite; a program needn't handle non-finite values.
Results may differ from a plain program's by a relative error of at most 0.02.
Values may be sent and summed in bfloat16 or wider, within the bound.
A program may use at most 128 MiB of HBM per device.

v0:
```python
from functools import partial

import jax
import jax.numpy as jnp
from jax import lax
from jax.sharding import PartitionSpec as P

HEAD_DIM = 64
TOP = 8


EPSILON = 1e-06
RESIDUAL = 0.22
SCORE_SCALE = 0.015625
NEGATIVE = -1e30


def rms_scale(values):
    return lax.rsqrt(jnp.mean(values * values, axis=-1, keepdims=True) + EPSILON)


def normed(values, gain_vec):
    return values * rms_scale(values) * gain_vec


def rotary_tables(length, head_width):
    half_width = head_width // 2
    frequency = 10000.0 ** (-2.0 * jnp.arange(half_width, dtype=jnp.float32) / head_width)
    angles = jnp.arange(length, dtype=jnp.float32)[:, None] * frequency[None, :]
    return (jnp.cos(angles), jnp.sin(angles))


def rotate(values, cosine, sine_table):
    half_width = values.shape[-1] // 2
    first_half = values[..., :half_width]
    second_half = values[..., half_width:]
    cos_b = cosine[:, None, :]
    sin_b = sine_table[:, None, :]
    return jnp.concatenate(
        [first_half * cos_b - second_half * sin_b, second_half * cos_b + first_half * sin_b],
        axis=-1,
    )


def attention_probs(scores):
    length = scores.shape[-1]
    causal = jnp.arange(length)[:, None] >= jnp.arange(length)[None, :]
    return jax.nn.softmax(jnp.where(causal, scores, NEGATIVE), axis=-1)


def swiglu(gate_up):
    half_width = gate_up.shape[-1] // 2
    return jax.nn.silu(gate_up[..., :half_width]) * gate_up[..., half_width:]


def softmax_last(values):
    return jax.nn.softmax(values, axis=-1)


def capacity(tokens, experts):
    return min(tokens, tokens * TOP * 5 // (4 * experts))


def left_product(left_rows, right_rows):
    return lax.dot_general(
        left_rows, right_rows, (((0,), (0,)), ((), ())), preferred_element_type=jnp.float32
    )


def right_transposed(left_rows, weight):
    return lax.dot_general(
        left_rows, weight, (((1,), (1,)), ((), ())), preferred_element_type=jnp.float32
    )


def shards(
    hidden_in,
    norm_attn,
    w_query,
    w_key,
    w_value,
    w_out,
    norm_ffn,
    w_router,
    w_gate_up,
    w_down,
    routes,
    out_grad,
):
    gain_attn, query_w, key_w, value_w, output_w, gain_ffn, router_w = (
        lax.all_gather(norm_attn, "shard", axis=0, tiled=True),
        lax.all_gather(w_query, "shard", axis=0, tiled=True),
        lax.all_gather(w_key, "shard", axis=0, tiled=True),
        lax.all_gather(w_value, "shard", axis=0, tiled=True),
        lax.all_gather(w_out, "shard", axis=0, tiled=True),
        lax.all_gather(norm_ffn, "shard", axis=0, tiled=True),
        lax.all_gather(w_router, "shard", axis=0, tiled=True),
    )
    tokens = hidden_in.shape[0]
    model_width = hidden_in.shape[1]
    kv_heads = key_w.shape[1] // HEAD_DIM
    q_heads = query_w.shape[1] // HEAD_DIM
    groups = q_heads // kv_heads
    n_expert = lax.axis_size("expert")
    experts = n_expert * w_gate_up.shape[0]
    slot_count = capacity(tokens, experts)
    cosine, sine_table = rotary_tables(tokens, HEAD_DIM)
    turning = partial(rotate, cosine=cosine, sine_table=sine_table)
    inputs = hidden_in.astype(jnp.float32)
    normed_one, norm_one_back = jax.vjp(normed, inputs, gain_attn.astype(jnp.float32))
    xn_one = normed_one.astype(jnp.bfloat16)
    raw_query = jnp.dot(xn_one, query_w, preferred_element_type=jnp.float32).reshape(
        tokens, q_heads, HEAD_DIM
    )
    raw_key = jnp.dot(xn_one, key_w, preferred_element_type=jnp.float32).reshape(
        tokens, kv_heads, HEAD_DIM
    )
    rot_query, query_back = jax.vjp(turning, raw_query)
    rot_key, key_back = jax.vjp(turning, raw_key)
    query_low = rot_query.astype(jnp.bfloat16).reshape(tokens, kv_heads, groups, HEAD_DIM)
    key_low = rot_key.astype(jnp.bfloat16)
    value_low = (
        jnp.dot(xn_one, value_w, preferred_element_type=jnp.float32)
        .astype(jnp.bfloat16)
        .reshape(tokens, kv_heads, HEAD_DIM)
    )
    scores = SCORE_SCALE * jnp.einsum(
        "tkgd,skd->kgts", query_low, key_low, preferred_element_type=jnp.float32
    )
    weights_low = attention_probs(scores).astype(jnp.bfloat16)
    attended = jnp.einsum(
        "kgts,skd->tkgd", weights_low, value_low, preferred_element_type=jnp.float32
    )
    attended = attended.reshape(tokens, q_heads * HEAD_DIM).astype(jnp.bfloat16)
    branch = jnp.dot(attended, output_w, preferred_element_type=jnp.float32)
    middle = inputs + RESIDUAL * branch
    normed_two, norm_two_back = jax.vjp(normed, middle, gain_ffn.astype(jnp.float32))
    xn_two = normed_two.astype(jnp.bfloat16)
    logits = jnp.dot(xn_two, router_w, preferred_element_type=jnp.float32)
    picked = jnp.take_along_axis(logits, routes, axis=1)
    gate_values, gate_back = jax.vjp(softmax_last, picked)
    flat_routes = routes.reshape(-1)
    row_count = flat_routes.shape[0]
    onehot_table = (flat_routes[:, None] == jnp.arange(experts, dtype=jnp.int32)[None, :]).astype(
        jnp.int32
    )
    row_ranks = jnp.sum((jnp.cumsum(onehot_table, axis=0) - 1) * onehot_table, axis=1)
    slot_index = flat_routes * slot_count + row_ranks
    slot_rows = (
        jnp.full((experts * slot_count,), row_count, jnp.int32)
        .at[slot_index]
        .set(jnp.arange(row_count, dtype=jnp.int32))
    )
    padded_tokens = jnp.concatenate([xn_two, jnp.zeros((1, model_width), jnp.bfloat16)], axis=0)
    send_rows = padded_tokens[slot_rows // TOP].reshape(experts, slot_count, model_width)
    received = lax.all_to_all(send_rows, "expert", split_axis=0, concat_axis=1, tiled=True)
    gate_up = jnp.einsum("erd,edf->erf", received, w_gate_up, preferred_element_type=jnp.float32)
    hidden_act, hidden_back = jax.vjp(swiglu, gate_up)
    hidden_low = hidden_act.astype(jnp.bfloat16)
    expert_out = jnp.einsum(
        "erf,efd->erd", hidden_low, w_down, preferred_element_type=jnp.float32
    ).astype(jnp.bfloat16)
    returned = lax.all_to_all(
        expert_out, "expert", split_axis=1, concat_axis=0, tiled=True
    ).reshape(experts * slot_count, model_width)
    chosen_low = returned[slot_index].reshape(tokens, TOP, model_width)
    mixture = jnp.einsum("tk,tkd->td", gate_values, chosen_low, preferred_element_type=jnp.float32)
    output = (middle + RESIDUAL * mixture).astype(jnp.bfloat16)
    upstream = out_grad.astype(jnp.float32)
    scaled_up = RESIDUAL * upstream
    gate_grad = jnp.einsum("tkd,td->tk", chosen_low, scaled_up, preferred_element_type=jnp.float32)
    row_grads = (
        (gate_values[:, :, None] * scaled_up[:, None, :])
        .astype(jnp.bfloat16)
        .reshape(row_count, model_width)
    )
    padded_grads = jnp.concatenate([row_grads, jnp.zeros((1, model_width), jnp.bfloat16)], axis=0)
    send_grads = padded_grads[slot_rows].reshape(experts, slot_count, model_width)
    grad_received = lax.all_to_all(send_grads, "expert", split_axis=0, concat_axis=1, tiled=True)
    hidden_grad = jnp.einsum(
        "erd,efd->erf", grad_received, w_down, preferred_element_type=jnp.float32
    )
    (gate_up_grad,) = hidden_back(hidden_grad)
    gate_up_low = gate_up_grad.astype(jnp.bfloat16)
    row_back = jnp.einsum(
        "erf,edf->erd", gate_up_low, w_gate_up, preferred_element_type=jnp.float32
    ).astype(jnp.bfloat16)
    down_local = jnp.einsum(
        "erf,erd->efd", hidden_low, grad_received, preferred_element_type=jnp.float32
    )
    gate_up_local = jnp.einsum(
        "erd,erf->edf", received, gate_up_low, preferred_element_type=jnp.float32
    )
    gate_up_sum, down_sum = (
        lax.psum_scatter(
            gate_up_local.astype(jnp.bfloat16), "shard", scatter_dimension=2, tiled=True
        ).astype(jnp.float32),
        lax.psum_scatter(
            down_local.astype(jnp.bfloat16), "shard", scatter_dimension=2, tiled=True
        ).astype(jnp.float32),
    )
    back_rows = lax.all_to_all(row_back, "expert", split_axis=1, concat_axis=0, tiled=True).reshape(
        experts * slot_count, model_width
    )
    token_grad = jnp.sum(
        back_rows[slot_index].reshape(tokens, TOP, model_width), axis=1, dtype=jnp.float32
    )
    (picked_grad,) = gate_back(gate_grad)
    compare = routes[:, :, None] == jnp.arange(experts, dtype=jnp.int32)[None, None, :]
    logit_grad = jnp.sum(jnp.where(compare, picked_grad[:, :, None], 0.0), axis=1).astype(
        jnp.bfloat16
    )
    xn_two_grad = token_grad + right_transposed(logit_grad, router_w)
    middle_part, gain_two_grad = norm_two_back(xn_two_grad)
    middle_grad = upstream + middle_part
    branch_low = (RESIDUAL * middle_grad).astype(jnp.bfloat16)
    attended_grad = right_transposed(branch_low, output_w).astype(jnp.bfloat16)
    attended_grad = attended_grad.reshape(tokens, kv_heads, groups, HEAD_DIM)
    scores_again = SCORE_SCALE * jnp.einsum(
        "tkgd,skd->kgts", query_low, key_low, preferred_element_type=jnp.float32
    )
    weights_again, probs_back = jax.vjp(attention_probs, scores_again)
    weights_again_low = weights_again.astype(jnp.bfloat16)
    value_grad = jnp.einsum(
        "kgts,tkgd->skd", weights_again_low, attended_grad, preferred_element_type=jnp.float32
    )
    value_grad = value_grad.astype(jnp.bfloat16).reshape(tokens, kv_heads * HEAD_DIM)
    probs_grad = jnp.einsum(
        "tkgd,skd->kgts", attended_grad, value_low, preferred_element_type=jnp.float32
    )
    (score_grad,) = probs_back(probs_grad)
    score_low = score_grad.astype(jnp.bfloat16)
    query_grad = SCORE_SCALE * jnp.einsum(
        "kgts,skd->tkgd", score_low, key_low, preferred_element_type=jnp.float32
    )
    key_grad = SCORE_SCALE * jnp.einsum(
        "kgts,tkgd->skd", score_low, query_low, preferred_element_type=jnp.float32
    )
    (query_raw_grad,) = query_back(query_grad.reshape(tokens, q_heads, HEAD_DIM))
    (key_raw_grad,) = key_back(key_grad)
    query_low_grad = query_raw_grad.reshape(tokens, q_heads * HEAD_DIM).astype(jnp.bfloat16)
    key_low_grad = key_raw_grad.reshape(tokens, kv_heads * HEAD_DIM).astype(jnp.bfloat16)
    xn_one_grad = right_transposed(query_low_grad, query_w)
    xn_one_grad = xn_one_grad + right_transposed(key_low_grad, key_w)
    xn_one_grad = xn_one_grad + right_transposed(value_grad, value_w)
    input_part, gain_one_grad = norm_one_back(xn_one_grad)
    input_grad = (middle_grad + input_part).astype(jnp.bfloat16)
    query_local = left_product(xn_one, query_low_grad)
    key_local = left_product(xn_one, key_low_grad)
    value_local = left_product(xn_one, value_grad)
    output_local = left_product(attended, branch_low)
    router_local = left_product(xn_two, logit_grad)
    (
        gain_one_piece,
        query_piece,
        key_piece,
        value_piece,
        output_piece,
        gain_two_piece,
        router_piece,
    ) = (
        lax.psum_scatter(
            gain_one_grad.astype(jnp.bfloat16), "shard", scatter_dimension=0, tiled=True
        ).astype(jnp.float32),
        lax.psum_scatter(
            query_local.astype(jnp.bfloat16), "shard", scatter_dimension=0, tiled=True
        ).astype(jnp.float32),
        lax.psum_scatter(
            key_local.astype(jnp.bfloat16), "shard", scatter_dimension=0, tiled=True
        ).astype(jnp.float32),
        lax.psum_scatter(
            value_local.astype(jnp.bfloat16), "shard", scatter_dimension=0, tiled=True
        ).astype(jnp.float32),
        lax.psum_scatter(
            output_local.astype(jnp.bfloat16), "shard", scatter_dimension=0, tiled=True
        ).astype(jnp.float32),
        lax.psum_scatter(
            gain_two_grad.astype(jnp.bfloat16), "shard", scatter_dimension=0, tiled=True
        ).astype(jnp.float32),
        lax.psum_scatter(
            router_local.astype(jnp.bfloat16), "shard", scatter_dimension=0, tiled=True
        ).astype(jnp.float32),
    )
    gain_one_sum, query_sum, key_sum, value_sum, output_sum, gain_two_sum, router_sum = (
        lax.psum(gain_one_piece.astype(jnp.bfloat16), "expert").astype(jnp.float32),
        lax.psum(query_piece.astype(jnp.bfloat16), "expert").astype(jnp.float32),
        lax.psum(key_piece.astype(jnp.bfloat16), "expert").astype(jnp.float32),
        lax.psum(value_piece.astype(jnp.bfloat16), "expert").astype(jnp.float32),
        lax.psum(output_piece.astype(jnp.bfloat16), "expert").astype(jnp.float32),
        lax.psum(gain_two_piece.astype(jnp.bfloat16), "expert").astype(jnp.float32),
        lax.psum(router_piece.astype(jnp.bfloat16), "expert").astype(jnp.float32),
    )
    return (
        output,
        input_grad,
        gain_one_sum,
        query_sum,
        key_sum,
        value_sum,
        output_sum,
        gain_two_sum,
        router_sum,
        gate_up_sum,
        down_sum,
    )


def solution(mesh):
    placed = (
        P(("expert", "shard"), None),
        P("shard"),
        P("shard", None),
        P("shard", None),
        P("shard", None),
        P("shard", None),
        P("shard"),
        P("shard", None),
        P("expert", None, None),
        P("expert", None, None),
        P(("expert", "shard"), None),
        P(("expert", "shard"), None),
    )
    return jax.shard_map(
        shards,
        mesh=mesh,
        in_specs=placed,
        out_specs=(
            P(("expert", "shard"), None),
            P(("expert", "shard"), None),
            P("shard"),
            P("shard", None),
            P("shard", None),
            P("shard", None),
            P("shard", None),
            P("shard"),
            P("shard", None),
            P("expert", None, "shard"),
            P("expert", None, "shard"),
        ),
        check_vma=False,
    )
```

profile of v0, /device:TPU:9, one launch (start us, length us, event | category | flops | bytes accessed | tf_op | source)
XLA Modules:
  0.0 784.0 jit_solution(13960970284539111894)
XLA Ops:
  33.9 21.2 %all-gather.9.cloned.1.call-done = bf16[1024,512]{1,0:T(8,128)(2,1)} async-done(((bf16[512,512]{1,0:T(8,128)(2,1)}), bf16[1024,512]{1,0:T(8,128)(2,1)}) %all-gather.9.cloned.1.call-update) | async-done | bytes 1048592 | tf_op jit(solution)/shard_map/all_gather | solution.py:93
  57.6 32.2 %all-gather.11.cloned.1.call-done = bf16[1024,1024]{1,0:T(8,128)(2,1)} async-done(((bf16[512,1024]{1,0:T(8,128)(2,1)}), bf16[1024,1024]{1,0:T(8,128)(2,1)}) %all-gather.11.cloned.1.call-update) | async-done | bytes 2097168 | tf_op jit(solution)/shard_map/all_gather | solution.py:92
  96.7 27.6 %all-gather.13.cloned.1.call-done = bf16[1024,1024]{1,0:T(8,128)(2,1)} async-done(((bf16[512,1024]{1,0:T(8,128)(2,1)}), bf16[1024,1024]{1,0:T(8,128)(2,1)}) %all-gather.13.cloned.1.call-update) | async-done | bytes 2097168 | tf_op jit(solution)/shard_map/all_gather | solution.py:95
  153.4 8.6 %gather_fusion.2 = bf16[1280,1024]{1,0:T(8,128)(2,1)} fusion(bf16[1025,1024]{1,0:T(8,128)(2,1)} %concatenate.24, s32[2048]{0:T(1024)S(1)} %copy-done.51), kind=kCustom, calls=%fused_computation.2 | custom fusion | bytes 5248000 | tf_op jit(solution)/shard_map/gather | solution.py:178
  162.0 34.0 %all-to-all-done = bf16[16,80,1024]{2,1,0:T(8,128)(2,1)} async-done(((bf16[16,80,1024]{2,1,0:T(8,128)(2,1)}), bf16[16,80,1024]{2,1,0:T(8,128)(2,1)}, u32[]{:S(2)}, u32[]{:S(2)}) %all-to-all-start) | async-done | bytes 2621472 | tf_op jit(solution)/shard_map/all_to_all | solution.py:156
  196.0 7.5 all-to-all-start.2
  209.8 50.1 %all-to-all-done.2 = bf16[16,80,1024]{2,1,0:T(8,128)(2,1)} async-done(((bf16[16,80,1024]{2,1,0:T(8,128)(2,1)}), bf16[16,80,1024]{2,1,0:T(8,128)(2,1)}, u32[]{:S(2)}, u32[]{:S(2)}) %all-to-all-start.2) | async-done | bytes 2621472 | tf_op jit(solution)/shard_map/all_to_all | solution.py:179
  270.4 18.2 %copy.170 = bf16[1,1280,1024]{2,0,1:T(2,128)(2,1)} copy(bf16[1,1280,1024]{2,1,0:T(8,128)(2,1)S(1)} %fusion.3) | data formatting | bytes 5242880 | tf_op jit(solution)/shard_map/convert_element_type | solution.py:187
  289.2 17.0 %reduce = bf16[1280,1024]{1,0:T(8,128)(2,1)} reduce(bf16[1280,1,1024]{2,1,0:T(2,128)(2,1)} %bitcast.205, bf16[]{:T(256)} %broadcast.315), dimensions={1}, to_apply=%bitcast.200.reduce_sub_computation | reduce | bytes 5242882
  313.5 7.8 all-to-all-start.3
  324.1 18.2 %copy.171 = bf16[1,1280,1024]{2,0,1:T(2,128)(2,1)} copy(bf16[1,1280,1024]{2,1,0:T(8,128)(2,1)S(1)} %fusion.2) | data formatting | bytes 5242880 | tf_op jit(solution)/shard_map/convert_element_type | solution.py:162
  342.3 17.1 %reduce.1 = bf16[1280,1024]{1,0:T(8,128)(2,1)} reduce(bf16[1280,1,1024]{2,1,0:T(2,128)(2,1)} %bitcast.206, bf16[]{:T(256)} %broadcast.315), dimensions={1}, to_apply=%bitcast.201.reduce_sub_computation | reduce | bytes 5242882
  366.6 11.1 %all-to-all-done.3 = bf16[16,2,40960]{2,1,0:T(2,128)(2,1)} async-done(((bf16[16,2,40960]{2,1,0:T(2,128)(2,1)}), bf16[16,2,40960]{2,1,0:T(2,128)(2,1)}, u32[]{:S(2)}, u32[]{:S(2)}) %all-to-all-start.3) | async-done | bytes 2621472 | tf_op jit(solution)/shard_map/all_to_all | solution.py:202
  387.1 11.0 %reshape.398 = bf16[1280,1,1024]{2,1,0:T(2,128)(2,1)} reshape(bf16[16,2,40960]{2,1,0:T(2,128)(2,1)} %all-to-all-done.3) | data formatting | bytes 5242880
  411.6 29.9 %all-to-all-done.1 = bf16[16,2,40960]{2,1,0:T(2,128)(2,1)} async-done(((bf16[16,2,40960]{2,1,0:T(2,128)(2,1)}), bf16[16,2,40960]{2,1,0:T(2,128)(2,1)}, u32[]{:S(2)}, u32[]{:S(2)}) %all-to-all-start.1) | async-done | bytes 2621472 | tf_op jit(solution)/shard_map/all_to_all | solution.py:163
  441.4 11.0 %reshape.396 = bf16[1280,1,1024]{2,1,0:T(2,128)(2,1)} reshape(bf16[16,2,40960]{2,1,0:T(2,128)(2,1)} %all-to-all-done.1) | data formatting | bytes 5242880
  494.3 7.6 convert_bitcast_fusion
  502.9 21.7 %reduce-scatter.10.cloned.1.call-done = bf16[512,512]{1,0:T(8,128)(2,1)} async-done(((bf16[1024,512]{1,0:T(8,128)(2,1)}), bf16[512,512]{1,0:T(8,128)(2,1)}) %reduce-scatter.10.cloned.1.call-update) | async-done | bytes 524304 | tf_op jit(solution)/shard_map/reduce_scatter | solution.py:268
  524.7 34.7 %reduce-scatter.14.cloned.1.call-done = bf16[512,1024]{1,0:T(8,128)(2,1)} async-done(((bf16[1024,1024]{1,0:T(8,128)(2,1)}), bf16[512,1024]{1,0:T(8,128)(2,1)}) %reduce-scatter.14.cloned.1.call-update) | async-done | bytes 1048592 | tf_op jit(solution)/shard_map/reduce_scatter | solution.py:274
  559.3 34.8 %reduce-scatter.8.cloned.1.call-done = bf16[512,1024]{1,0:T(8,128)(2,1)} async-done(((bf16[1024,1024]{1,0:T(8,128)(2,1)}), bf16[512,1024]{1,0:T(8,128)(2,1)}) %reduce-scatter.8.cloned.1.call-update) | async-done | bytes 1048592 | tf_op jit(solution)/shard_map/reduce_scatter | solution.py:265
  595.4 21.9 %reduce-scatter.20.cloned.1.call-done = bf16[1,512,512]{2,1,0:T(8,128)(2,1)} async-done(((bf16[1,512,1024]{2,1,0:T(8,128)(2,1)}), bf16[1,512,512]{2,1,0:T(8,128)(2,1)}) %reduce-scatter.20.cloned.1.call-update) | async-done | bytes 524304 | tf_op jit(solution)/shard_map/reduce_scatter | solution.py:198
  619.4 32.5 %reduce-scatter.18.cloned.1.call-done = bf16[1,1024,512]{2,1,0:T(8,128)(2,1)} async-done(((bf16[1,1024,1024]{2,1,0:T(8,128)(2,1)}), bf16[1,1024,512]{2,1,0:T(8,128)(2,1)}) %reduce-scatter.18.cloned.1.call-update) | async-done | bytes 1048592 | tf_op jit(solution)/shard_map/reduce_scatter | solution.py:195
  664.1 49.7 %all-reduce.10 = (bf16[512]{0:T(512)(128)(2,1)S(1)}, bf16[512]{0:T(512)(128)(2,1)S(1)}, bf16[512,16]{0,1:T(8,128)(2,1)S(1)}) all-reduce(bf16[512]{0:T(512)(128)(2,1)S(1)} %dynamic-slice.1, bf16[512]{0:T(512)(128)(2,1)S(1)} %dynamic-slice.3, ...), channel_id=1, replica_groups=mesh['expert'=16,'shard'=2] {'expert'}, use_global_device_ids=true, to_apply=%region_18.19 | all-reduce | flops 9216 | bytes 36864 | tf_op jit(solution)/shard_map/psum | solution.py:285
  715.6 54.6 %all-reduce.15.cloned.1.call-done = (bf16[512,1024]{1,0:T(8,128)(2,1)}, bf16[512,512]{1,0:T(8,128)(2,1)}, bf16[512,512]{1,0:T(8,128)(2,1)}, bf16[512,1024]{1,0:T(8,128)(2,1)}) async-done(((bf16[512,1024]{1,0:T(8,128)(2,1)}, bf16[512,512]{1,0:T(8,128)(2,1)}, bf16[512,512]{1,0:T(8,128)(2,1)}, bf16[512,1024]{1,0:T(8,128)(2,1)}), (bf16[512,1024]{1,0:T(8,128)(2,1)}, bf16[512,512]{1,0:T(8,128)(2,1)}, ...) | async-done | bytes 3145744 | tf_op jit(solution)/shard_map/psum | solution.py:286
  (294 shorter events, 187.7 us)
Async XLA Ops:
  7.2 196.3 %copy-start = (bf16[1,1024,1024]{2,1,0:T(8,128)(2,1)S(1)}, bf16[1,1024,1024]{2,1,0:T(8,128)(2,1)}, u32[]{:S(2)}) copy-start(bf16[1,1024,1024]{2,1,0:T(8,128)(2,1)} %param.20) | copy-start | bytes 6291460
  7.2 25.0 %all-gather.7.cloned.1.call-start = ((), (), s32[]{:S(2)}) async-start(), calls=%async_computation.11 | async-start | bytes 1572864 | tf_op jit(solution)/shard_map/all_gather | solution.py:94
  8.0 47.1 %all-gather.9.cloned.1.call-start = ((), (), s32[]{:S(2)}) async-start(), calls=%async_computation.12 | async-start | bytes 1572864 | tf_op jit(solution)/shard_map/all_gather | solution.py:93
  8.7 81.1 %all-gather.11.cloned.1.call-start = ((), (), s32[]{:S(2)}) async-start(), calls=%async_computation.13 | async-start | bytes 3145728 | tf_op jit(solution)/shard_map/all_gather | solution.py:92
  9.5 114.9 %all-gather.13.cloned.1.call-start = ((), (), s32[]{:S(2)}) async-start(), calls=%async_computation.14 | async-start | bytes 3145728 | tf_op jit(solution)/shard_map/all_gather | solution.py:95
  11.1 81.3 %copy-start.52 = (f32[128]{0:T(128)}, f32[128]{0:T(128)S(1)}, u32[]{:S(2)}) copy-start(f32[128]{0:T(128)S(1)} %fusion.59) | copy-start | bytes 1540
  11.6 80.8 %copy-start.30 = (f32[128,32]{0,1:T(8,128)}, f32[128,32]{0,1:T(8,128)S(1)}, u32[]{:S(2)}) copy-start(f32[128,32]{0,1:T(8,128)S(1)} %get-tuple-element.42) | copy-start | bytes 49156
  28.9 97.8 %copy-start.47 = (f32[2,1,512]{2,1,0:T(1,128)}, f32[2,1,512]{2,1,0:T(1,128)S(1)}, u32[]{:S(2)}) copy-start(f32[2,1,512]{2,1,0:T(1,128)S(1)} %convert_element_type.235) | copy-start | bytes 12292
  132.8 63.1 %all-to-all-start = ((bf16[16,80,1024]{2,1,0:T(8,128)(2,1)}), bf16[16,80,1024]{2,1,0:T(8,128)(2,1)}, u32[]{:S(2)}, u32[]{:S(2)}) async-start(bf16[16,80,1024]{2,1,0:T(8,128)(2,1)} %bitcast.209), calls=%async_computation | async-start | bytes 5242880 | tf_op jit(solution)/shard_map/all_to_all | solution.py:156
  151.2 234.6 %copy-start.40 = (f32[128,8]{0,1:T(8,128)}, f32[128,8]{0,1:T(8,128)S(1)}, u32[]{:S(2)}) copy-start(f32[128,8]{0,1:T(8,128)S(1)} %get-tuple-element.25) | copy-start | bytes 12292
  151.2 234.6 %copy-start.55 = (f32[128]{0:T(128)}, f32[128]{0:T(128)S(1)}, u32[]{:S(2)}) copy-start(f32[128]{0:T(128)S(1)} %get-tuple-element.24) | copy-start | bytes 1540
  151.3 235.3 %copy-start.60 = (f32[128]{0:T(128)}, f32[128]{0:T(128)S(1)}, u32[]{:S(2)}) copy-start(f32[128]{0:T(128)S(1)} %fusion.56) | copy-start | bytes 1540
  196.0 64.0 %all-to-all-start.2 = ((bf16[16,80,1024]{2,1,0:T(8,128)(2,1)}), bf16[16,80,1024]{2,1,0:T(8,128)(2,1)}, u32[]{:S(2)}, u32[]{:S(2)}) async-start(bf16[16,80,1024]{2,1,0:T(8,128)(2,1)} %bitcast.210), calls=%async_computation.2 | async-start | bytes 5242880 | tf_op jit(solution)/shard_map/all_to_all | solution.py:179
  313.5 64.3 %all-to-all-start.3 = ((bf16[16,2,40960]{2,1,0:T(2,128)(2,1)}), bf16[16,2,40960]{2,1,0:T(2,128)(2,1)}, u32[]{:S(2)}, u32[]{:S(2)}) async-start(bf16[16,2,40960]{2,1,0:T(2,128)(2,1)} %reshape.397), calls=%async_computation.3 | async-start | bytes 5242880 | tf_op jit(solution)/shard_map/all_to_all | solution.py:202
  377.8 63.7 %all-to-all-start.1 = ((bf16[16,2,40960]{2,1,0:T(2,128)(2,1)}), bf16[16,2,40960]{2,1,0:T(2,128)(2,1)}, u32[]{:S(2)}, u32[]{:S(2)}) async-start(bf16[16,2,40960]{2,1,0:T(2,128)(2,1)} %reshape.395), calls=%async_computation.1 | async-start | bytes 5242880 | tf_op jit(solution)/shard_map/all_to_all | solution.py:163
  384.8 118.1 %reduce-scatter.12.cloned.1.call-start = ((), (), s32[]{:S(2)}) async-start(), calls=%async_computation.17 | async-start | bytes 1572864 | tf_op jit(solution)/shard_map/reduce_scatter | solution.py:271
  480.4 44.3 %reduce-scatter.10.cloned.1.call-start = ((), (), s32[]{:S(2)}) async-start(), calls=%async_computation.16 | async-start | bytes 1572864 | tf_op jit(solution)/shard_map/reduce_scatter | solution.py:268
  485.0 74.3 %reduce-scatter.14.cloned.1.call-start = ((), (), s32[]{:S(2)}) async-start(), calls=%async_computation.18 | async-start | bytes 3145728 | tf_op jit(solution)/shard_map/reduce_scatter | solution.py:274
  487.1 107.0 %reduce-scatter.8.cloned.1.call-start = ((), (), s32[]{:S(2)}) async-start(), calls=%async_computation.15 | async-start | bytes 3145728 | tf_op jit(solution)/shard_map/reduce_scatter | solution.py:265
  489.9 127.4 %reduce-scatter.20.cloned.1.call-start = ((), (), s32[]{:S(2)}) async-start(), calls=%async_computation.21 | async-start | bytes 1572864 | tf_op jit(solution)/shard_map/reduce_scatter | solution.py:198
  494.3 157.6 %reduce-scatter.18.cloned.1.call-start = ((), (), s32[]{:S(2)}) async-start(), calls=%async_computation.20 | async-start | bytes 3145728 | tf_op jit(solution)/shard_map/reduce_scatter | solution.py:195
  502.0 92.2 %copy-start.67 = (u32[32]{0:T(128)S(1)}, u32[32]{0:T(128)}, u32[]{:S(2)}) copy-start(u32[32]{0:T(128)} %constant.123) | copy-start | bytes 388
  502.0 162.1 %reduce-scatter.16.cloned.1.call-start = ((), (), s32[]{:S(2)}) async-start(), calls=%async_computation.19 | async-start | bytes 49152 | tf_op jit(solution)/shard_map/reduce_scatter | solution.py:280
  502.9 267.3 %all-reduce.15.cloned.1.call-start = ((), (), s32[]{:S(2)}) async-start(), calls=%async_computation.22 | async-start | bytes 6291456 | tf_op jit(solution)/shard_map/psum | solution.py:286
  (62 other events, 600.8 us)
Sparse Core Ops, SparseCore 0:
  9.6 22.5 all-gather.6
  33.7 21.2 all-gather.8
  56.6 33.1 all-gather.10
  91.2 33.1 all-gather.12
  480.5 20.9 reduce-scatter.11
  504.3 20.3 reduce-scatter.9
  527.5 31.8 reduce-scatter.13
  562.2 31.8 reduce-scatter.7
  596.9 20.3 reduce-scatter.19
  620.0 31.8 reduce-scatter.17
  654.7 9.3 reduce-scatter.15
  667.8 102.3 all-reduce.14
where the time goes:
time: 796 us; the launch traced here: 784 us
  waiting for transfers between devices  415 us (52%)
  local copies, waits for them, and re-layouts  132 us (17%)
  other arithmetic  64.8 us (8%)
  blocking collectives  64.2 us (8%)
  matrix products  62 us (8%)
  starting transfers between devices  29.7 us (4%)
  between operations  16.3 us (2%)
    psum x1, waiting for transfers between devices, shards(): lax.psum(query_piece.astype(jnp.bfloat16), 'expert').astype(jnp.float32)  54.6 us
    unnamed x153, local copies, waits for them, and re-layouts  50.7 us
    all_to_all x1, waiting for transfers between devices, shards(): lax.all_to_all(send_grads, 'expert', split_axis=0, concat_axis=1, tiled=T...  50.1 us
    psum x1, blocking collectives, shards(): lax.psum(gain_one_piece.astype(jnp.bfloat16), 'expert').astype(jnp.float32)  49.7 us
    reduce_scatter x1, waiting for transfers between devices, shards(): lax.psum_scatter(query_local.astype(jnp.bfloat16), 'shard', scatter_dimen...  34.8 us
    reduce_scatter x1, waiting for transfers between devices, shards(): lax.psum_scatter(output_local.astype(jnp.bfloat16), 'shard', scatter_dime...  34.7 us
    unnamed x2, other arithmetic  34.1 us
    all_to_all x1, waiting for transfers between devices, shards(): lax.all_to_all(send_rows, 'expert', split_axis=0, concat_axis=1, tiled=True)  34 us
  transfers between devices with their start and end apart: 16, of which 15 were waited for; matrix products, arithmetic and copies ran while one was open for 19% of the time, Pallas kernels for 0%

commit v1 on v0

v1 whole, which is shorter than its diff:
```python
from functools import partial

import jax
import jax.numpy as jnp
from jax import lax
from jax.sharding import PartitionSpec as P

HEAD_DIM = 64
EPSILON = 1e-06
RESIDUAL = 0.22
SCORE_SCALE = 0.015625
NEGATIVE = -1e30
F32 = jnp.float32
BF16 = jnp.bfloat16


def rms_scale(values):
    return lax.rsqrt(jnp.mean(values * values, axis=-1, keepdims=True) + EPSILON)


def rotary_tables(length, head_width):
    half_width = head_width // 2
    frequency = 10000.0 ** (-2.0 * jnp.arange(half_width, dtype=F32) / head_width)
    angles = jnp.arange(length, dtype=F32)[:, None] * frequency[None, :]
    return (jnp.cos(angles), jnp.sin(angles))


def rotate(values, cosine, sine_table):
    half_width = values.shape[-1] // 2
    first_half = values[..., :half_width]
    second_half = values[..., half_width:]
    cos_b = cosine[:, None, :]
    sin_b = sine_table[:, None, :]
    return jnp.concatenate(
        [first_half * cos_b - second_half * sin_b, second_half * cos_b + first_half * sin_b],
        axis=-1,
    )


def attention_probs(scores):
    length = scores.shape[-1]
    causal = jnp.arange(length)[:, None] >= jnp.arange(length)[None, :]
    return jax.nn.softmax(jnp.where(causal, scores, NEGATIVE), axis=-1)


def product(left, right):
    return jnp.dot(left, right, preferred_element_type=F32)


def left_product(left_rows, right_rows):
    return lax.dot_general(
        left_rows, right_rows, (((0,), (0,)), ((), ())), preferred_element_type=F32
    )


def right_transposed(left_rows, weight):
    return lax.dot_general(
        left_rows, weight, (((1,), (1,)), ((), ())), preferred_element_type=F32
    )


def shift(values, step):
    n = lax.axis_size("shard")
    return lax.ppermute(values, "shard", [(i, (i + step) % n) for i in range(n)])


def piece(values, index, axis):
    n = lax.axis_size("shard")
    width = values.shape[axis] // n
    return lax.dynamic_slice_in_dim(values, lax.rem(index, n) * width, width, axis)


def rows_of_all(values):
    n = lax.axis_size("shard")
    return jnp.concatenate([values] + [shift(values, d) for d in range(1, n)], axis=0)


def columns_of_all(values):
    n, me = lax.axis_size("shard"), lax.axis_index("shard")
    parts = [piece(values, me, 1)]
    parts += [shift(piece(values, me + d, 1), d) for d in range(1, n)]
    return jnp.concatenate(parts, axis=0)


def sum_home(partial_rows):
    n = lax.axis_size("shard")
    rows = partial_rows.shape[0] // n
    total = partial_rows[:rows]
    for d in range(1, n):
        total = total + shift(partial_rows[d * rows : (d + 1) * rows].astype(BF16), -d).astype(F32)
    return total


def columns_home(values):
    n, me = lax.axis_size("shard"), lax.axis_index("shard")
    rows, width = values.shape[0] // n, values.shape[1]
    parts = [values[:rows]]
    parts += [shift(values[d * rows : (d + 1) * rows], -d) for d in range(1, n)]
    if n == 2:
        return jnp.where(
            me == 0, jnp.concatenate(parts, axis=1), jnp.concatenate(parts[::-1], axis=1)
        )
    return jnp.roll(jnp.concatenate(parts, axis=1), me * width, axis=1)


def sum_pieces(values, axis, sent=BF16):
    n, me = lax.axis_size("shard"), lax.axis_index("shard")
    total = piece(values, me, axis)
    for d in range(1, n):
        total = total + shift(piece(values, me + d, axis).astype(sent), d).astype(F32)
    return total


def shards(
    hidden_in,
    norm_attn,
    w_query,
    w_key,
    w_value,
    w_out,
    norm_ffn,
    w_router,
    w_gate_up,
    w_down,
    routes,
    out_grad,
):
    tokens, model_width = hidden_in.shape
    kv_heads = w_key.shape[1] // HEAD_DIM
    q_heads = w_query.shape[1] // HEAD_DIM
    groups = q_heads // kv_heads
    q_width, kv_width = w_query.shape[1], w_key.shape[1]
    experts = w_router.shape[1]
    w_gu, w_dn = w_gate_up[0], w_down[0]
    ffn = w_dn.shape[0]

    small = lax.all_gather(
        jnp.concatenate([w_router, norm_ffn[:, None]], axis=1), "shard", axis=0, tiled=True
    )
    router_w, gain_two = small[:, :experts], small[:, experts].astype(F32)
    mask = jnp.any(
        routes[:, :, None] == jnp.arange(experts, dtype=jnp.int32)[None, None, :], axis=1
    )
    mask_all = lax.all_gather(mask.astype(BF16), "expert", axis=0, tiled=True)
    og_all = lax.all_gather(out_grad, "expert", axis=0, tiled=True)

    cosine, sine_table = rotary_tables(tokens, HEAD_DIM)
    turning = partial(rotate, cosine=cosine, sine_table=sine_table)
    inputs = hidden_in.astype(F32)
    r1 = rms_scale(inputs)
    gain_one = norm_attn.astype(F32)
    hidden_cols = columns_of_all(hidden_in).astype(F32)
    scaled_cols = hidden_cols * rows_of_all(r1)
    xn_one = (scaled_cols * gain_one).astype(BF16)
    qkv = sum_home(
        jnp.concatenate(
            [product(xn_one, w_query), product(xn_one, w_key), product(xn_one, w_value)], axis=1
        )
    )
    raw_query = qkv[:, :q_width].reshape(tokens, q_heads, HEAD_DIM)
    raw_key = qkv[:, q_width : q_width + kv_width].reshape(tokens, kv_heads, HEAD_DIM)
    value_low = qkv[:, q_width + kv_width :].astype(BF16).reshape(tokens, kv_heads, HEAD_DIM)
    rot_query, query_back = jax.vjp(turning, raw_query)
    rot_key, key_back = jax.vjp(turning, raw_key)
    query_low = rot_query.astype(BF16).reshape(tokens, kv_heads, groups, HEAD_DIM)
    key_low = rot_key.astype(BF16)
    scores = SCORE_SCALE * jnp.einsum(
        "tkgd,skd->kgts", query_low, key_low, preferred_element_type=F32
    )
    probs, probs_back = jax.vjp(attention_probs, scores)
    probs_low = probs.astype(BF16)
    attended = jnp.einsum("kgts,skd->tkgd", probs_low, value_low, preferred_element_type=F32)
    attended = attended.reshape(tokens, q_heads * HEAD_DIM).astype(BF16)
    attended_cols = columns_of_all(attended)
    middle = inputs + RESIDUAL * sum_home(product(attended_cols, w_out))
    r2 = rms_scale(middle)
    xn_two = (middle * r2 * gain_two).astype(BF16)

    x_all = lax.all_gather(xn_two, "expert", axis=0, tiled=True)
    logits_all = jnp.where(mask_all > 0, product(x_all, router_w), NEGATIVE)
    gates_all = jax.nn.softmax(logits_all, axis=-1)
    mine = jnp.arange(experts, dtype=jnp.int32) == lax.axis_index("expert")
    gate = jnp.sum(jnp.where(mine, gates_all, 0.0), axis=-1, keepdims=True)
    gate_up = product(x_all, w_gu)
    g, u = gate_up[:, :ffn], gate_up[:, ffn:]
    sig = jax.nn.sigmoid(g)
    hid = (g * sig * u).astype(BF16)
    y = product(hid, w_dn).astype(BF16).astype(F32)
    mixture = lax.psum_scatter(
        (gate * y).astype(BF16), "expert", scatter_dimension=0, tiled=True
    )
    og_scaled = RESIDUAL * og_all.astype(F32)
    dy = (gate * og_scaled).astype(BF16)
    gate_grad_col = jnp.sum(y * og_scaled, axis=-1).reshape(experts, tokens)
    gate_grad = lax.all_to_all(gate_grad_col, "expert", split_axis=0, concat_axis=0, tiled=True).T
    dhid = right_transposed(dy, w_dn)
    dgu = jnp.concatenate(
        [dhid * u * sig * (1.0 + g * (1.0 - sig)), dhid * g * sig], axis=1
    ).astype(BF16)
    token_grad = lax.psum_scatter(
        right_transposed(dgu, w_gu).astype(BF16), "expert", scatter_dimension=0, tiled=True
    ).astype(F32)
    down_sum = sum_pieces(left_product(hid, dy), 1)
    gate_up_sum = sum_pieces(left_product(x_all, dgu), 1)

    output = (middle + RESIDUAL * mixture.astype(F32)).astype(BF16)
    upstream = out_grad.astype(F32)
    gates = jax.nn.softmax(
        jnp.where(mask, product(xn_two, router_w), NEGATIVE), axis=-1
    )
    gate_grad = jnp.where(mask, gate_grad, 0.0)
    logit_grad = (
        gates * (gate_grad - jnp.sum(gates * gate_grad, axis=-1, keepdims=True))
    ).astype(BF16)
    xn_two_grad = token_grad + right_transposed(logit_grad, router_w)
    scaled_two = middle * r2
    gain_two_grad = jnp.sum(xn_two_grad * scaled_two, axis=0)
    w2 = xn_two_grad * gain_two
    middle_grad = (
        upstream + r2 * (w2 - scaled_two * jnp.mean(w2 * scaled_two, axis=-1, keepdims=True))
    )
    branch_low = (RESIDUAL * middle_grad).astype(BF16)
    router_local = left_product(xn_two, logit_grad)
    branch_all = rows_of_all(branch_low)
    attended_grad = columns_home(right_transposed(branch_all, w_out).astype(BF16))
    output_local = left_product(attended_cols, branch_all).astype(BF16)
    small_local = sum_pieces(
        jnp.concatenate([router_local, gain_two_grad[:, None]], axis=1), 0, F32
    ).astype(BF16)
    small_rows = -(-(experts + 1) // 16) * 16
    small_pad = jnp.pad(
        small_local.T,
        ((0, small_rows - experts - 1), (0, model_width - small_local.shape[0])),
    )
    first_sum = lax.psum(jnp.concatenate([output_local, small_pad], axis=0), "expert").astype(F32)

    attended_grad = attended_grad.reshape(tokens, kv_heads, groups, HEAD_DIM)
    value_grad = jnp.einsum(
        "kgts,tkgd->skd", probs_low, attended_grad, preferred_element_type=F32
    )
    probs_grad = jnp.einsum(
        "tkgd,skd->kgts", attended_grad, value_low, preferred_element_type=F32
    )
    (score_grad,) = probs_back(probs_grad)
    score_low = score_grad.astype(BF16)
    query_grad = SCORE_SCALE * jnp.einsum(
        "kgts,skd->tkgd", score_low, key_low, preferred_element_type=F32
    )
    key_grad = SCORE_SCALE * jnp.einsum(
        "kgts,tkgd->skd", score_low, query_low, preferred_element_type=F32
    )
    (query_raw_grad,) = query_back(query_grad.reshape(tokens, q_heads, HEAD_DIM))
    (key_raw_grad,) = key_back(key_grad)
    qkv_grad = jnp.concatenate(
        [
            query_raw_grad.reshape(tokens, q_width).astype(BF16),
            key_raw_grad.reshape(tokens, kv_width).astype(BF16),
            value_grad.reshape(tokens, kv_width).astype(BF16),
        ],
        axis=1,
    )
    qkv_all = rows_of_all(qkv_grad)
    xn_one_grad = (
        right_transposed(qkv_all[:, :q_width], w_query)
        + right_transposed(qkv_all[:, q_width : q_width + kv_width], w_key)
        + right_transposed(qkv_all[:, q_width + kv_width :], w_value)
    )
    gain_one_grad = jnp.sum(xn_one_grad * scaled_cols, axis=0)
    second = left_product(xn_one, qkv_all).astype(BF16)
    gain_pad = jnp.pad(
        gain_one_grad.astype(BF16)[None, :],
        ((0, 15), (0, second.shape[1] - gain_one_grad.shape[0])),
    )
    second_sum = lax.psum(jnp.concatenate([second, gain_pad], axis=0), "expert").astype(F32)
    w1 = columns_home((xn_one_grad * gain_one).astype(BF16)).astype(F32)
    scaled_one = inputs * r1
    input_grad = (
        middle_grad + r1 * (w1 - scaled_one * jnp.mean(w1 * scaled_one, axis=-1, keepdims=True))
    ).astype(BF16)

    own = norm_attn.shape[0]
    return (
        output,
        input_grad,
        second_sum[own, :own],
        second_sum[:own, :q_width],
        second_sum[:own, q_width : q_width + kv_width],
        second_sum[:own, q_width + kv_width :],
        first_sum[:own],
        first_sum[own + experts, :own],
        first_sum[own : own + experts, :own].T,
        gate_up_sum[None],
        down_sum[None],
    )


def solution(mesh):
    placed = (
        P(("expert", "shard"), None),
        P("shard"),
        P("shard", None),
        P("shard", None),
        P("shard", None),
        P("shard", None),
        P("shard"),
        P("shard", None),
        P("expert", None, None),
        P("expert", None, None),
        P(("expert", "shard"), None),
        P(("expert", "shard"), None),
    )
    return jax.shard_map(
        shards,
        mesh=mesh,
        in_specs=placed,
        out_specs=(
            P(("expert", "shard"), None),
            P(("expert", "shard"), None),
            P("shard"),
            P("shard", None),
            P("shard", None),
            P("shard", None),
            P("shard", None),
            P("shard"),
            P("shard", None),
            P("expert", None, "shard"),
            P("expert", None, "shard"),
        ),
        check_vma=False,
    )
```

time: 796 us -> 447 us (0.56)
  waiting for transfers between devices: 415 us -> 275 us
  local copies, waits for them, and re-layouts: 132 us -> 23.6 us
  other arithmetic: 64.8 us -> 21.2 us
  blocking collectives: 64.2 us -> 29.2 us
  starting transfers between devices: 29.7 us -> 12.7 us
    all_to_all x4 -> x1, waiting for transfers between devices: 125 us -> 0.01 us  [shards(): lax.all_to_all(gate_grad_col, 'expert', split_axis=0, concat_axis=0, tile...]
    reduce_scatter x7 -> x2, waiting for transfers between devices: 148 us -> 61.4 us  [the longest x1 44.7 us: shards(): lax.psum_scatter(right_transposed(dgu, w_gu).astype(BF16), 'expert', scat...]
    psum x1, waiting for transfers between devices: 54.6 us -> 106 us  [shards(): lax.psum(jnp.concatenate([second, gain_pad], axis=0), 'expert').astype(F32)]
    psum x1 -> x0, blocking collectives: 49.7 us -> none  [shards(): lax.psum(gain_one_piece.astype(jnp.bfloat16), 'expert').astype(jnp.float32)]
    unnamed x153 -> x98, local copies, waits for them, and re-layouts: 50.7 us -> 4.91 us
    ppermute x0 -> x12, waiting for transfers between devices: none -> 35.5 us  [shift(): lax.ppermute(values, 'shard', [(i, (i + step) % n) for i in range(n)])]
    gather x9 -> x0, local copies, waits for them, and re-layouts: 35.3 us -> none  [the longest x1 8.6 us: shards(): padded_grads[slot_rows].reshape(experts, slot_count, model_width)]
    unnamed x2 -> x0, other arithmetic: 34.1 us -> none
  transfers between devices with their start and end apart: 16 -> 18, of which waited for: 15 -> 11; matrix products, arithmetic and copies ran while one was open for 19% -> 15% of each run, Pallas kernels for 0% -> 0%
where the time goes in v1:
time: 447 us; the launch traced here: 443 us
  waiting for transfers between devices  275 us (62%)
  matrix products  66.4 us (15%)
  blocking collectives  29.2 us (7%)
  local copies, waits for them, and re-layouts  23.6 us (5%)
  other arithmetic  21.2 us (5%)
  between operations  14.6 us (3%)
  starting transfers between devices  12.7 us (3%)
    psum x1, waiting for transfers between devices, shards(): lax.psum(jnp.concatenate([second, gain_pad], axis=0), 'expert').astype(F32)  106 us
    reduce_scatter x1, waiting for transfers between devices, shards(): lax.psum_scatter(right_transposed(dgu, w_gu).astype(BF16), 'expert', scat...  44.7 us
    all_gather x1, waiting for transfers between devices, shards(): og_all = lax.all_gather(out_grad, 'expert', axis=0, tiled=True)  40.6 us
    ppermute x12, waiting for transfers between devices, shift(): lax.ppermute(values, 'shard', [(i, (i + step) % n) for i in range(n)])  35.5 us
    all_gather x1, waiting for transfers between devices, shards(): x_all = lax.all_gather(xn_two, 'expert', axis=0, tiled=True)  30.3 us
    dot_general x8, matrix products, product(): return jnp.dot(left, right, preferred_element_type=F32)  24.2 us
    all_gather x1, blocking collectives, shards(): mask_all = lax.all_gather(mask.astype(BF16), 'expert', axis=0, tiled=True)  24.1 us
    dot_general x5, matrix products, left_product(): lax.dot_general(left_rows, right_rows, (((0,), (0,)), ((), ())), preferre...  18.4 us
  transfers between devices with their start and end apart: 18, of which 11 were waited for; matrix products, arithmetic and copies ran while one was open for 15% of the time, Pallas kernels for 0%

profile of v1, /device:TPU:9, one launch (start us, length us, event | category | flops | bytes accessed | tf_op | source)
XLA Modules:
  0.0 442.7 jit_solution(6994408272203694028)
XLA Ops:
  19.1 10.5 %collective-permute-done.2 = bf16[128,2048]{1,0:T(8,128)(2,1)S(1)} collective-permute-done((bf16[128,2048]{1,0:T(8,128)(2,1)S(1)}, bf16[128,2048]{1,0:T(8,128)(2,1)S(1)}, u32[]{:S(2)}, u32[]{:S(2)}) %collective-permute-start.2) | collective-permute-done | bytes 524320 | tf_op jit(solution)/shard_map/ppermute | solution.py:64
  33.3 2.2 fusion.89
  37.7 2.8 collective-permute-done.3
  43.3 5.1 %all_gather.13 = bf16[1024,17]{0,1:T(8,128)(2,1)S(1)} all-gather(bf16[512,17]{0,1:T(8,128)(2,1)S(1)} %pad_maximum_fusion.20), channel_id=1, replica_groups=mesh['expert'=16,'shard'=2] {'shard'}, dimensions={0}, use_global_device_ids=true | all-gather | bytes 52224 | tf_op jit(solution)/shard_map/all_gather | solution.py:137
  52.0 24.1 %all_gather.12 = bf16[2048,16]{0,1:T(8,128)(2,1)S(1)} all-gather(bf16[128,16]{0,1:T(8,128)(2,1)S(1)} %convert_element_type.182), channel_id=1, replica_groups=mesh['expert'=16,'shard'=2] {'expert'}, dimensions={0}, use_global_device_ids=true | all-gather | bytes 69632 | tf_op jit(solution)/shard_map/all_gather | solution.py:144
  76.1 30.3 %all-gather.3.cloned.1.call-done = bf16[2048,1024]{1,0:T(8,128)(2,1)} async-done(((bf16[128,1024]{1,0:T(8,128)(2,1)}), bf16[2048,1024]{1,0:T(8,128)(2,1)}) %all-gather.3.cloned.1.call-update) | async-done | bytes 4194320 | tf_op jit(solution)/shard_map/all_gather | solution.py:179
  106.5 3.5 fusion.90
  110.2 6.9 %fusion.9 = f32[2048,1024]{0,1:T(8,128)} fusion(bf16[2048,1024]{1,0:T(8,128)(2,1)S(1)} %copy-done.6, bf16[1,1024,1024]{2,1,0:T(8,128)(2,1)S(1)} %copy-done), kind=kOutput, calls=%fused_computation.25 | convolution fusion | flops 4294967296 | bytes 14680064 | tf_op jit(solution)/shard_map/dot_general | solution.py:47
  117.1 40.6 %all-gather.5.cloned.1.call-done = bf16[2048,1024]{1,0:T(8,128)(2,1)} async-done(((bf16[128,1024]{1,0:T(8,128)(2,1)}), bf16[2048,1024]{1,0:T(8,128)(2,1)}) %all-gather.5.cloned.1.call-update) | async-done | bytes 4194320 | tf_op jit(solution)/shard_map/all_gather | solution.py:145
  157.7 8.9 %multiply_convert_fusion.1 = (bf16[2048,512]{0,1:T(8,128)(2,1)S(1)}, bf16[2048,512]{0,1:T(8,128)(2,1)S(1)}, bf16[2048,512]{0,1:T(8,128)(2,1)}) fusion(f32[2048,1024]{0,1:T(8,128)} %fusion.9, bf16[1,512,1024]{2,1,0:T(8,128)(2,1)} %param.21, bf16[2048,1024]{1,0:T(8,128)(2,1)} %all-gather.5.cloned.1.call-done, f32[2048]{0:T(1024)S(1)} %broadcast_multiply_fusion), kind=kOutput, calls=%fused_computation.12 | convolution fusion | flops 2170552320 | bytes 19931136 | tf_op jit(solution)/shard_map/dot_general | solution.py:57
  168.6 6.3 %convolution_convert_fusion.1 = bf16[2048,1024]{1,0:T(8,128)(2,1)} fusion(bf16[2048,512]{0,1:T(8,128)(2,1)S(1)} %get-tuple-element.18, bf16[2048,512]{0,1:T(8,128)(2,1)S(1)} %get-tuple-element.17, bf16[1,1024,1024]{2,1,0:T(8,128)(2,1)S(1)} %copy-done), kind=kOutput, calls=%fused_computation.16 | convolution fusion | flops 4305453056 | bytes 10485760 | tf_op jit(solution)/shard_map/dot_general | solution.py:57
  176.3 8.4 %fusion.2 = (f32[2048]{0:T(1024)}, bf16[2048,1024]{1,0:T(8,128)(2,1)}) fusion(bf16[2048,1024]{1,0:T(8,128)(2,1)} %all-gather.5.cloned.1.call-done, f32[2048]{0:T(1024)S(1)} %select_reduce_fusion, bf16[2048,512]{0,1:T(8,128)(2,1)} %get-tuple-element.19, bf16[1,512,1024]{2,1,0:T(8,128)(2,1)S(1)} %copy-done.44), kind=kOutput, calls=%fused_computation.6 | convolution fusion | flops 2164258816 | bytes 11550720 | tf_op jit(solution)/shard_map/dot_general | solution.py:47
  184.7 3.7 all-to-all-start
  188.5 6.9 %fusion.11 = f32[512,1024]{1,0:T(8,128)} fusion(bf16[2048,512]{0,1:T(8,128)(2,1)} %get-tuple-element.19, bf16[2048,1024]{1,0:T(8,128)(2,1)} %all-gather.5.cloned.1.call-done, f32[2048]{0:T(1024)S(1)} %broadcast_multiply_fusion), kind=kOutput, calls=%fused_computation.29 | convolution fusion | flops 2153775104 | bytes 8396800 | tf_op jit(solution)/shard_map/dot_general | solution.py:51
  199.0 44.7 %reduce-scatter.5.cloned.1.call-done = bf16[128,1024]{1,0:T(8,128)(2,1)} async-done(((bf16[2048,1024]{1,0:T(8,128)(2,1)}), bf16[128,1024]{1,0:T(8,128)(2,1)}) %reduce-scatter.5.cloned.1.call-update) | async-done | bytes 262160 | tf_op jit(solution)/shard_map/reduce_scatter | solution.py:200
  246.6 10.1 %fusion.5 = f32[1024,1024]{1,0:T(8,128)} fusion(bf16[2048,1024]{1,0:T(8,128)(2,1)} %all-gather.3.cloned.1.call-done, bf16[2048,512]{0,1:T(8,128)(2,1)} %copy-done.48, bf16[2048,512]{0,1:T(8,128)(2,1)} %copy-done.47), kind=kOutput, calls=%fused_computation.18 | convolution fusion | flops 4303355904 | bytes 12582912 | tf_op jit(solution)/shard_map/dot_general | solution.py:51
  267.2 2.8 dynamic-slice_convert_fusion
  273.6 3.1 collective-permute-done.7
  280.7 2.5 add_bitcast_fusion.1
  283.7 15.6 %collective-permute-done.10 = bf16[1024,512]{1,0:T(8,128)(2,1)} collective-permute-done((bf16[1024,512]{1,0:T(8,128)(2,1)}, bf16[1024,512]{1,0:T(8,128)(2,1)}, u32[]{:S(2)}, u32[]{:S(2)}) %collective-permute-start.10) | collective-permute-done | bytes 1048608 | tf_op jit(solution)/shard_map/ppermute | solution.py:64
  299.3 3.6 add_bitcast_fusion
  303.1 16.7 %reduce-scatter.3.cloned.1.call-done = bf16[128,1024]{1,0:T(8,128)(2,1)} async-done(((bf16[2048,1024]{1,0:T(8,128)(2,1)}), bf16[128,1024]{1,0:T(8,128)(2,1)}) %reduce-scatter.3.cloned.1.call-update) | async-done | bytes 262160 | tf_op jit(solution)/shard_map/reduce_scatter | solution.py:189
  321.7 106.2 %all-reduce.9.cloned.1.call-done = (bf16[528,2048]{1,0:T(8,128)(2,1)}, bf16[544,1024]{1,0:T(8,128)(2,1)}) async-done(((bf16[528,2048]{1,0:T(8,128)(2,1)}, bf16[544,1024]{1,0:T(8,128)(2,1)}), (bf16[528,2048]{1,0:T(8,128)(2,1)}, bf16[544,1024]{1,0:T(8,128)(2,1)})) %all-reduce.9.cloned.1.call-update) | async-done | bytes 3276816 | tf_op jit(solution)/shard_map/psum | solution.py:274
  428.0 3.0 fusion.86
  (214 shorter events, 59.4 us)
Async XLA Ops:
  7.2 103.0 %copy-start = (bf16[1,1024,1024]{2,1,0:T(8,128)(2,1)S(1)}, bf16[1,1024,1024]{2,1,0:T(8,128)(2,1)}, u32[]{:S(2)}) copy-start(bf16[1,1024,1024]{2,1,0:T(8,128)(2,1)} %param.20) | copy-start | bytes 6291460
  7.2 99.3 %all-gather.3.cloned.1.call-start = ((), (), s32[]{:S(2)}) async-start(), calls=%async_computation.3 | async-start | bytes 4456448 | tf_op jit(solution)/shard_map/all_gather | solution.py:179
  8.5 5.6 %collective-permute-start = (bf16[128,512]{1,0:T(8,128)(2,1)S(1)}, bf16[128,512]{1,0:T(8,128)(2,1)S(1)}, u32[]{:S(2)}, u32[]{:S(2)}) collective-permute-start(bf16[128,512]{1,0:T(8,128)(2,1)S(1)} %get-tuple-element.43), channel_id=1, source_target_pairs={{0,1},{1,0},{2,3},{3,2},{4,5},{5,4},{6,7},{7,6},{8,9},{9,8},{10,11... | collective-permute-start | bytes 393224 | tf_op jit(solution)/shard_map/ppermute | solution.py:64
  11.4 2.6 collective-permute-start.1
  17.9 11.6 %collective-permute-start.2 = (bf16[128,2048]{1,0:T(8,128)(2,1)S(1)}, bf16[128,2048]{1,0:T(8,128)(2,1)S(1)}, u32[]{:S(2)}, u32[]{:S(2)}) collective-permute-start(bf16[128,2048]{1,0:T(8,128)(2,1)S(1)} %slice.178), channel_id=1, source_target_pairs={{0,1},{1,0},{2,3},{3,2},{4,5},{5,4},{6,7},{7,6},{8,9},{9,8},{10,11... | collective-permute-start | bytes 1572872 | tf_op jit(solution)/shard_map/ppermute | solution.py:64
  36.6 3.9 collective-permute-start.3
  42.9 6.2 %collective-permute-start.4 = (bf16[128,1024]{1,0:T(8,128)(2,1)S(1)}, bf16[128,1024]{1,0:T(8,128)(2,1)S(1)}, u32[]{:S(2)}, u32[]{:S(2)}) collective-permute-start(bf16[128,1024]{1,0:T(8,128)(2,1)S(1)} %slice.179), channel_id=1, source_target_pairs={{0,1},{1,0},{2,3},{3,2},{4,5},{5,4},{6,7},{7,6},{8,9},{9,8},{10,11... | collective-permute-start | bytes 786440 | tf_op jit(solution)/shard_map/ppermute | solution.py:64
  49.3 195.8 %copy-start.39 = (f32[128]{0:T(128)}, f32[128]{0:T(128)S(1)}, u32[]{:S(2)}) copy-start(f32[128]{0:T(128)S(1)} %add_rsqrt_fusion) | copy-start | bytes 1540
  50.5 107.2 %all-gather.5.cloned.1.call-start = ((), (), s32[]{:S(2)}) async-start(), calls=%async_computation.5 | async-start | bytes 4456448 | tf_op jit(solution)/shard_map/all_gather | solution.py:145
  51.3 192.5 %reduce-scatter.5.cloned.1.call-start = ((), (), s32[]{:S(2)}) async-start(), calls=%async_computation.6 | async-start | bytes 4456448 | tf_op jit(solution)/shard_map/reduce_scatter | solution.py:200
  184.7 14.3 %all-to-all-start = ((f32[16,1,128]{2,1,0:T(1,128)}), f32[16,1,128]{2,1,0:T(1,128)S(1)}, u32[]{:S(2)}, u32[]{:S(2)}) async-start(f32[16,1,128]{2,1,0:T(1,128)} %bitcast.18), calls=%async_computation.2 | async-start | bytes 16384 | tf_op jit(solution)/shard_map/all_to_all | solution.py:195
  188.4 131.3 %reduce-scatter.3.cloned.1.call-start = ((), (), s32[]{:S(2)}) async-start(), calls=%async_computation.4 | async-start | bytes 4456448 | tf_op jit(solution)/shard_map/reduce_scatter | solution.py:189
  195.4 48.4 %copy-start.33 = (f32[1024,1]{0,1:T(1,128)S(1)}, f32[1024,1]{0,1:T(1,128)}, u32[]{:S(2)}) copy-start(f32[1024,1]{0,1:T(1,128)} %copy-done.32) | copy-start | bytes 12292
  195.4 49.7 %copy-start.9 = (bf16[128,1024]{1,0:T(8,128)(2,1)S(1)}, bf16[128,1024]{1,0:T(8,128)(2,1)}, u32[]{:S(2)}) copy-start(bf16[128,1024]{1,0:T(8,128)(2,1)} %param.23) | copy-start | bytes 786436
  197.5 83.2 %collective-permute-start.11 = (bf16[512,512]{1,0:T(8,128)(2,1)}, bf16[512,512]{1,0:T(8,128)(2,1)}, u32[]{:S(2)}, u32[]{:S(2)}) collective-permute-start(bf16[512,512]{1,0:T(8,128)(2,1)} %dynamic-slice_convert_fusion.1), channel_id=1, source_target_pairs={{0,1},{1,0},{2,3},{3,2},{4,5},{5,4},{6,7},{7,6},{8,9},{9,8},{10,11... | collective-permute-start | bytes 1572872 | tf_op jit(solution)/shard_map/ppermute | solution.py:64
  198.7 229.3 %all-reduce.9.cloned.1.call-start = ((), (), s32[]{:S(2)}) async-start(), calls=%async_computation.7 | async-start | bytes 6553600 | tf_op jit(solution)/shard_map/psum | solution.py:274
  245.4 11.3 %collective-permute-start.5 = (bf16[128,1024]{1,0:T(8,128)(2,1)S(1)}, bf16[128,1024]{1,0:T(8,128)(2,1)S(1)}, u32[]{:S(2)}, u32[]{:S(2)}) collective-permute-start(bf16[128,1024]{1,0:T(8,128)(2,1)S(1)} %multiply_convert_fusion.4), channel_id=1, source_target_pairs={{0,1},{1,0},{2,3},{3,2},{4,5},{5,4},{6,7},{7,6},{8,9},{9,8},{10,11... | collective-permute-start | bytes 786440 | tf_op jit(solution)/shard_map/ppermute | solution.py:64
  257.9 4.1 collective-permute-start.6
  259.0 12.1 %collective-permute-start.9 = (f32[512,17]{0,1:T(8,128)}, f32[512,17]{0,1:T(8,128)}, u32[]{:S(2)}, u32[]{:S(2)}) collective-permute-start(f32[512,17]{0,1:T(8,128)} %fusion.53), channel_id=1, source_target_pairs={{0,1},{1,0},{2,3},{3,2},{4,5},{5,4},{6,7},{7,6},{8,9},{9,8},{10,11... | collective-permute-start | bytes 104456 | tf_op jit(solution)/shard_map/ppermute | solution.py:64
  266.8 9.9 %collective-permute-start.7 = (bf16[128,2048]{0,1:T(8,128)(2,1)S(1)}, bf16[128,2048]{0,1:T(8,128)(2,1)S(1)}, u32[]{:S(2)}, u32[]{:S(2)}) collective-permute-start(bf16[128,2048]{0,1:T(8,128)(2,1)S(1)} %pad_maximum_fusion.6), channel_id=1, source_target_pairs={{0,1},{1,0},{2,3},{3,2},{4,5},{5,4},{6,7},{7,6},{8,9},{9,8},{10,11... | collective-permute-start | bytes 1572872 | tf_op jit(solution)/shard_map/ppermute | solution.py:64
  270.0 29.3 %collective-permute-start.10 = (bf16[1024,512]{1,0:T(8,128)(2,1)}, bf16[1024,512]{1,0:T(8,128)(2,1)}, u32[]{:S(2)}, u32[]{:S(2)}) collective-permute-start(bf16[1024,512]{1,0:T(8,128)(2,1)} %dynamic-slice_convert_fusion), channel_id=1, source_target_pairs={{0,1},{1,0},{2,3},{3,2},{4,5},{5,4},{6,7},{7,6},{8,9},{9,8},{10,11... | collective-permute-start | bytes 3145736 | tf_op jit(solution)/shard_map/ppermute | solution.py:64
  280.6 22.2 %copy-start.43 = (f32[128]{0:T(128)S(1)}, f32[128]{0:T(128)}, u32[]{:S(2)}) copy-start(f32[128]{0:T(128)} %get-tuple-element.44) | copy-start | bytes 1540
  280.6 39.1 %copy-start.40 = (f32[128]{0:T(128)S(1)}, f32[128]{0:T(128)}, u32[]{:S(2)}) copy-start(f32[128]{0:T(128)} %copy-done.39) | copy-start | bytes 1540
  283.2 19.6 %collective-permute-start.8 = (bf16[128,512]{1,0:T(8,128)(2,1)S(1)}, bf16[128,512]{1,0:T(8,128)(2,1)S(1)}, u32[]{:S(2)}, u32[]{:S(2)}) collective-permute-start(bf16[128,512]{1,0:T(8,128)(2,1)S(1)} %get-tuple-element.36), channel_id=1, source_target_pairs={{0,1},{1,0},{2,3},{3,2},{4,5},{5,4},{6,7},{7,6},{8,9},{9,8},{10,11... | collective-permute-start | bytes 393224 | tf_op jit(solution)/shard_map/ppermute | solution.py:64
  (43 other events, 248.5 us)
Sparse Core Ops, SparseCore 0:
  50.6 55.7 all-gather.2
  108.6 49.0 all-gather.4
  175.1 68.6 reduce-scatter.4
  247.9 71.7 reduce-scatter.2
  323.8 104.1 all-reduce.8

commit v2 on v1

--- a/solution.py
+++ b/solution.py
@@ -3,6 +3,8 @@
 import jax
 import jax.numpy as jnp
 from jax import lax
+from jax.experimental import pallas as pl
+from jax.experimental.pallas import tpu as pltpu
 from jax.sharding import PartitionSpec as P
 
 HEAD_DIM = 64
@@ -73,6 +75,14 @@
 def rows_of_all(values):
     n = lax.axis_size("shard")
     return jnp.concatenate([values] + [shift(values, d) for d in range(1, n)], axis=0)
+
+
+def rows_in_order(values):
+    n, me = lax.axis_size("shard"), lax.axis_index("shard")
+    parts = [values] + [shift(values, -d) for d in range(1, n)]
+    if n == 2:
+        return jnp.where(me == 0, jnp.concatenate(parts), jnp.concatenate(parts[::-1]))
+    return jnp.roll(jnp.concatenate(parts), me * values.shape[0], axis=0)
 
 
 def columns_of_all(values):
@@ -109,6 +119,266 @@
     for d in range(1, n):
         total = total + shift(piece(values, me + d, axis).astype(sent), d).astype(F32)
     return total
+
+
+MESH = pl.DeviceIdType.MESH
+
+
+def grid_of(n):
+    return (4, n // 8) if n % 8 == 0 else (n // 2, 1)
+
+
+class Place:
+    def __init__(self, n):
+        self.outer, self.inner = grid_of(n)
+        me = lax.axis_index("expert")
+        self.me = me
+        self.core = lax.rem(me, 2)
+        self.b = lax.rem(me // 2, self.inner)
+        self.a = me // (2 * self.inner)
+
+    def index(self, da=0, db=0, dc=0):
+        a = lax.rem(self.a + da, self.outer)
+        b = lax.rem(self.b + db, self.inner)
+        return (a * self.inner + b) * 2 + lax.rem(self.core + dc, 2)
+
+    def barrier(self):
+        sem = pltpu.get_barrier_semaphore()
+        mates = [self.index(da=d) for d in range(1, self.outer)]
+        mates += [self.index(db=d) for d in range(1, self.inner)]
+        mates += [self.index(dc=1)]
+        for mate in mates:
+            pl.semaphore_signal(sem, inc=1, device_id={"expert": mate}, device_id_type=MESH)
+        pl.semaphore_wait(sem, len(mates))
+
+
+def remote(src, dst, send_sem, recv_sem, target):
+    return pltpu.make_async_remote_copy(
+        src_ref=src,
+        dst_ref=dst,
+        send_sem=send_sem,
+        recv_sem=recv_sem,
+        device_id={"expert": target},
+        device_id_type=MESH,
+    )
+
+
+def gather_steps(place, sources, outs, local_sem, send_sem, recv_sem):
+    outer, inner = place.outer, place.inner
+    items = range(len(sources))
+    started = []
+
+    def send(block, target, number, own=False):
+        for i in items:
+            src = sources[i] if own else outs[i].at[block]
+            copy = remote(
+                src, outs[i].at[block], send_sem.at[i, number], recv_sem.at[i, block], target
+            )
+            copy.start()
+            started.append(copy)
+
+    def arrived(block):
+        for i in items:
+            remote(
+                outs[i].at[block], outs[i].at[block], send_sem.at[i, 0], recv_sem.at[i, block], place.index(dc=1)
+            ).wait_recv()
+
+    number = 0
+    for d in range(1, outer):
+        send(place.me, place.index(da=d), number, True)
+        number += 1
+    for d in range(1, inner):
+        send(place.me, place.index(db=d), number, True)
+        number += 1
+    send(place.me, place.index(dc=1), number, True)
+    number += 1
+    local = [
+        pltpu.make_async_copy(sources[i], outs[i].at[place.me], local_sem.at[i]) for i in items
+    ]
+    for copy in local:
+        copy.start()
+    for da in range(1, outer):
+        block = place.index(da=da)
+        arrived(block)
+        for d in range(1, inner):
+            send(block, place.index(db=d), number)
+            number += 1
+        send(block, place.index(dc=1), number)
+        number += 1
+    for db in range(1, inner):
+        for da in range(outer):
+            block = place.index(da=da, db=db)
+            arrived(block)
+            send(block, place.index(dc=1), number)
+            number += 1
+    for da in range(outer):
+        for db in range(inner):
+            arrived(place.index(da=da, db=db, dc=1))
+    for copy in started:
+        copy.wait_send()
+    for copy in local:
+        copy.wait()
+
+
+def gather_sends(n):
+    outer, inner = grid_of(n)
+    return (outer - 1) + outer * (inner - 1) + outer * inner
+
+
+def scatter_steps(place, src, buf_c, buf_b, buf_a, sems):
+    outer, inner = place.outer, place.inner
+    send_c, recv_c, send_b, recv_b, send_a, recv_a = sems
+    far_first = list(range(1, outer)) + [0]
+    inner_order = list(range(1, inner)) + [0]
+    started = []
+
+    def across(da, db):
+        slot = place.index(da=da, db=db) // 2
+        return remote(
+            src.at[place.index(da=da, db=db, dc=1)],
+            buf_c.at[slot],
+            send_c.at[slot],
+            recv_c.at[slot],
+            place.index(dc=1),
+        )
+
+    def along_inner(da, db):
+        slot = place.index(da=da, db=db) // 2
+        a = lax.rem(place.a + da, outer)
+        return remote(
+            buf_c.at[slot],
+            buf_b.at[db - 1, a],
+            send_b.at[db - 1, a],
+            recv_b.at[db - 1, a],
+            place.index(db=db),
+        )
+
+    def along_outer(da):
+        slot = place.index(da=da) // 2
+        return remote(
+            buf_c.at[slot], buf_a.at[da - 1], send_a.at[da - 1], recv_a.at[da - 1], place.index(da=da)
+        )
+
+    def start(copy):
+        copy.start()
+        started.append(copy)
+
+    for db in inner_order:
+        for da in far_first:
+            start(across(da, db))
+    for db in inner_order:
+        for da in far_first:
+            slot = place.index(da=da, db=db) // 2
+            across(da, db).wait_recv()
+            block = place.index(da=da, db=db)
+            buf_c[slot] = (buf_c[slot].astype(F32) + src[block].astype(F32)).astype(BF16)
+            if db:
+                start(along_inner(da, db))
+    total = None
+    for da in far_first:
+        slot = place.index(da=da) // 2
+        a = lax.rem(place.a + da, outer)
+        total = buf_c[slot].astype(F32)
+        for db in range(1, inner):
+            along_inner(da, db).wait_recv()
+            total = total + buf_b[db - 1, a].astype(F32)
+        if da:
+            buf_c[slot] = total.astype(BF16)
+            start(along_outer(da))
+    for da in range(1, outer):
+        along_outer(da).wait_recv()
+        total = total + buf_a[da - 1].astype(F32)
+    for copy in started:
+        copy.wait_send()
+    return total
+
+
+def scatter_scratch(n, rows, width):
+    outer, inner = grid_of(n)
+    dma = pltpu.SemaphoreType.DMA
+    inner_slots = max(1, inner - 1)
+    return [
+        pltpu.VMEM((outer * inner, rows, width), BF16),
+        pltpu.VMEM((inner_slots, outer, rows, width), BF16),
+        pltpu.VMEM((outer - 1, rows, width), BF16),
+        dma((outer * inner,)),
+        dma((outer * inner,)),
+        dma((inner_slots, outer)),
+        dma((inner_slots, outer)),
+        dma((outer - 1,)),
+        dma((outer - 1,)),
+    ]
+
+
+def kernel_params(number):
+    return pltpu.CompilerParams(
+        collective_id=number, has_side_effects=True, vmem_limit_bytes=48 * 1024 * 1024
+    )
+
+
+def gather_kernel(n, count, *refs):
+    place = Place(n)
+    place.barrier()
+    gather_steps(place, refs[:count], refs[count : 2 * count], *refs[2 * count :])
+
+
+def gather_expert(arrays, number):
+    n, count = lax.axis_size("expert"), len(arrays)
+    dma = pltpu.SemaphoreType.DMA
+    outs = pl.pallas_call(
+        partial(gather_kernel, n, count),
+        out_shape=[jax.ShapeDtypeStruct((n,) + v.shape, v.dtype) for v in arrays],
+        in_specs=[pl.BlockSpec(memory_space=pl.ANY)] * count,
+        out_specs=[pl.BlockSpec(memory_space=pl.ANY)] * count,
+        scratch_shapes=[dma((count,)), dma((count, gather_sends(n))), dma((count, n))],
+        compiler_params=kernel_params(number),
+    )(*arrays)
+    return [out.reshape((-1,) + v.shape[1:]) for out, v in zip(outs, arrays)]
+
+
+def scatter_kernel(n, src, out, buf_c, buf_b, buf_a, *sems):
+    place = Place(n)
+    place.barrier()
+    out[...] = scatter_steps(place, src, buf_c, buf_b, buf_a, sems)
+
+
+def scatter_expert(values, number):
+    n = lax.axis_size("expert")
+    rows, width = values.shape[0] // n, values.shape[1]
+    return pl.pallas_call(
+        partial(scatter_kernel, n),
+        out_shape=jax.ShapeDtypeStruct((rows, width), F32),
+        in_specs=[pl.BlockSpec(memory_space=pltpu.VMEM)],
+        out_specs=pl.BlockSpec(memory_space=pltpu.VMEM),
+        scratch_shapes=scatter_scratch(n, rows, width),
+        compiler_params=kernel_params(number),
+    )(values.reshape(n, rows, width))
+
+
+def sum_kernel(n, src, out, own, buf_c, buf_b, buf_a, *sems):
+    place = Place(n)
+    place.barrier()
+    own[...] = scatter_steps(place, src, buf_c, buf_b, buf_a, sems[:6]).astype(BF16)
+    gather_steps(place, [own], [out], *sems[6:])
+
+
+def sum_expert(values, number):
+    n = lax.axis_size("expert")
+    dma = pltpu.SemaphoreType.DMA
+    whole_rows, width = values.shape
+    rows = -(-whole_rows // (16 * n)) * 16
+    values = jnp.pad(values, ((0, rows * n - whole_rows), (0, 0)))
+    out = pl.pallas_call(
+        partial(sum_kernel, n),
+        out_shape=jax.ShapeDtypeStruct((n, rows, width), BF16),
+        in_specs=[pl.BlockSpec(memory_space=pltpu.VMEM)],
+        out_specs=pl.BlockSpec(memory_space=pl.ANY),
+        scratch_shapes=[pltpu.VMEM((rows, width), BF16)]
+        + scatter_scratch(n, rows, width)
+        + [dma((1,)), dma((1, gather_sends(n))), dma((1, n))],
+        compiler_params=kernel_params(number),
+    )(values.reshape(n, rows, width))
+    return out.reshape(n * rows, width)[:whole_rows]
 
 
 def shards(
@@ -134,14 +404,11 @@
     w_gu, w_dn = w_gate_up[0], w_down[0]
     ffn = w_dn.shape[0]
 
-    small = lax.all_gather(
-        jnp.concatenate([w_router, norm_ffn[:, None]], axis=1), "shard", axis=0, tiled=True
-    )
+    small = rows_in_order(jnp.concatenate([w_router, norm_ffn[:, None]], axis=1))
     router_w, gain_two = small[:, :experts], small[:, experts].astype(F32)
     mask = jnp.any(
         routes[:, :, None] == jnp.arange(experts, dtype=jnp.int32)[None, None, :], axis=1
     )
-    mask_all = lax.all_gather(mask.astype(BF16), "expert", axis=0, tiled=True)
     og_all = lax.all_gather(out_grad, "expert", axis=0, tiled=True)
 
     cosine, sine_table = rotary_tables(tokens, HEAD_DIM)
@@ -176,7 +443,9 @@
     r2 = rms_scale(middle)
     xn_two = (middle * r2 * gain_two).astype(BF16)
 
-    x_all = lax.all_gather(xn_two, "expert", axis=0, tiled=True)
+    mask_pad = jnp.pad(mask.astype(BF16), ((0, 0), (0, -experts % 128)))
+    x_all, mask_all = gather_expert([xn_two, mask_pad], 1)
+    mask_all = mask_all[:, :experts]
     logits_all = jnp.where(mask_all > 0, product(x_all, router_w), NEGATIVE)
     gates_all = jax.nn.softmax(logits_all, axis=-1)
     mine = jnp.arange(experts, dtype=jnp.int32) == lax.axis_index("expert")
@@ -197,9 +466,7 @@
     dgu = jnp.concatenate(
         [dhid * u * sig * (1.0 + g * (1.0 - sig)), dhid * g * sig], axis=1
     ).astype(BF16)
-    token_grad = lax.psum_scatter(
-        right_transposed(dgu, w_gu).astype(BF16), "expert", scatter_dimension=0, tiled=True
-    ).astype(F32)
+    token_grad = scatter_expert(right_transposed(dgu, w_gu).astype(BF16), 2)
     down_sum = sum_pieces(left_product(hid, dy), 1)
     gate_up_sum = sum_pieces(left_product(x_all, dgu), 1)
 
@@ -226,13 +493,7 @@
     output_local = left_product(attended_cols, branch_all).astype(BF16)
     small_local = sum_pieces(
         jnp.concatenate([router_local, gain_two_grad[:, None]], axis=1), 0, F32
-    ).astype(BF16)
-    small_rows = -(-(experts + 1) // 16) * 16
-    small_pad = jnp.pad(
-        small_local.T,
-        ((0, small_rows - experts - 1), (0, model_width - small_local.shape[0])),
-    )
-    first_sum = lax.psum(jnp.concatenate([output_local, small_pad], axis=0), "expert").astype(F32)
+    )
 
     attended_grad = attended_grad.reshape(tokens, kv_heads, groups, HEAD_DIM)
     value_grad = jnp.einsum(
@@ -266,29 +527,33 @@
         + right_transposed(qkv_all[:, q_width + kv_width :], w_value)
     )
     gain_one_grad = jnp.sum(xn_one_grad * scaled_cols, axis=0)
-    second = left_product(xn_one, qkv_all).astype(BF16)
-    gain_pad = jnp.pad(
-        gain_one_grad.astype(BF16)[None, :],
-        ((0, 15), (0, second.shape[1] - gain_one_grad.shape[0])),
-    )
-    second_sum = lax.psum(jnp.concatenate([second, gain_pad], axis=0), "expert").astype(F32)
+    small_local = jnp.concatenate([small_local, gain_one_grad[:, None]], axis=1)
+    small_pad = jnp.pad(small_local, ((0, 0), (0, -small_local.shape[1] % 128)))
+    sums = sum_expert(
+        jnp.concatenate(
+            [left_product(xn_one, qkv_all).astype(BF16), output_local, small_pad.astype(BF16)],
+            axis=1,
+        ),
+        3,
+    ).astype(F32)
     w1 = columns_home((xn_one_grad * gain_one).astype(BF16)).astype(F32)
     scaled_one = inputs * r1
     input_grad = (
         middle_grad + r1 * (w1 - scaled_one * jnp.mean(w1 * scaled_one, axis=-1, keepdims=True))
     ).astype(BF16)
 
-    own = norm_attn.shape[0]
+    out_at = q_width + 2 * kv_width
+    small_at = out_at + model_width
     return (
         output,
         input_grad,
-        second_sum[own, :own],
-        second_sum[:own, :q_width],
-        second_sum[:own, q_width : q_width + kv_width],
-        second_sum[:own, q_width + kv_width :],
-        first_sum[:own],
-        first_sum[own + experts, :own],
-        first_sum[own : own + experts, :own].T,
+        sums[:, small_at + experts + 1],
+        sums[:, :q_width],
+        sums[:, q_width : q_width + kv_width],
+        sums[:, q_width + kv_width : out_at],
+        sums[:, out_at:small_at],
+        sums[:, small_at + experts],
+        sums[:, small_at : small_at + experts],
         gate_up_sum[None],
         down_sum[None],
     )

time: 447 us -> 364 us (0.81)
  waiting for transfers between devices: 275 us -> 57.7 us
  Pallas kernels: 0 us -> 159 us
  blocking collectives: 29.2 us -> 0 us
  local copies, waits for them, and re-layouts: 23.6 us -> 31.9 us
    pallas_call x0 -> x3, Pallas kernels: none -> 159 us  [the longest x1 68.2 us: sum_expert(): pl.pallas_call(partial(sum_kernel, n), out_shape=jax.ShapeDtypeStruct((n,...]
    psum x1 -> x0, waiting for transfers between devices: 106 us -> none  [shards(): lax.psum(jnp.concatenate([second, gain_pad], axis=0), 'expert').astype(F32)]
    reduce_scatter x1 -> x0, waiting for transfers between devices: 44.7 us -> none  [shards(): lax.psum_scatter(right_transposed(dgu, w_gu).astype(BF16), 'expert', scat...]
    all_gather x1, waiting for transfers between devices: 40.6 us -> 0.01 us  [shards(): og_all = lax.all_gather(out_grad, 'expert', axis=0, tiled=True)]
    all_gather x1 -> x0, waiting for transfers between devices: 30.3 us -> none  [shards(): x_all = lax.all_gather(xn_two, 'expert', axis=0, tiled=True)]
    all_gather x2 -> x0, blocking collectives: 29.2 us -> none  [the longest x1 24.1 us: shards(): mask_all = lax.all_gather(mask.astype(BF16), 'expert', axis=0, tiled=True)]
    ppermute x12 -> x13, waiting for transfers between devices: 35.5 us -> 57.7 us  [shift(): lax.ppermute(values, 'shard', [(i, (i + step) % n) for i in range(n)])]
    reduce_scatter x1, waiting for transfers between devices: 16.7 us -> 0.01 us  [shards(): lax.psum_scatter((gate * y).astype(BF16), 'expert', scatter_dimension=0,...]
  transfers between devices with their start and end apart: 18 -> 16, of which waited for: 11 -> 6; matrix products, arithmetic and copies ran while one was open for 15% -> 23% of each run, Pallas kernels for 0% -> 44%
where the time goes in v2:
time: 364 us; the launch traced here: 363 us
  Pallas kernels  159 us (44%)
  matrix products  64.7 us (18%)
  waiting for transfers between devices  57.7 us (16%)
  local copies, waits for them, and re-layouts  31.9 us (9%)
  other arithmetic  23.6 us (6%)
  between operations  15 us (4%)
  starting transfers between devices  11.3 us (3%)
    pallas_call x1, Pallas kernels, sum_expert(): pl.pallas_call(partial(sum_kernel, n), out_shape=jax.ShapeDtypeStruct((n,...  68.2 us
    ppermute x13, waiting for transfers between devices, shift(): lax.ppermute(values, 'shard', [(i, (i + step) % n) for i in range(n)])  57.7 us
    pallas_call x1, Pallas kernels, gather_expert(): pl.pallas_call(partial(gather_kernel, n, count), out_shape=[jax.ShapeDtyp...  54.3 us
    pallas_call x1, Pallas kernels, scatter_expert(): pl.pallas_call(partial(scatter_kernel, n), out_shape=jax.ShapeDtypeStruct...  36 us
    dot_general x8, matrix products, product(): return jnp.dot(left, right, preferred_element_type=F32)  22 us
    dot_general x7, matrix products, right_transposed(): lax.dot_general(left_rows, weight, (((1,), (1,)), ((), ())), preferred_el...  18.3 us
    dot_general x5, matrix products, left_product(): lax.dot_general(left_rows, right_rows, (((0,), (0,)), ((), ())), preferre...  17.4 us
    unnamed x101, local copies, waits for them, and re-layouts  9.88 us
  transfers between devices with their start and end apart: 16, of which 6 were waited for; matrix products, arithmetic and copies ran while one was open for 23% of the time, Pallas kernels for 44%

profile of v2, /device:TPU:9, one launch (start us, length us, event | category | flops | bytes accessed | tf_op | source)
XLA Modules:
  0.0 362.7 jit_solution(16173636505084360000)
XLA Ops:
  25.0 10.9 %collective-permute-done.2 = bf16[128,2048]{1,0:T(8,128)(2,1)S(1)} collective-permute-done((bf16[128,2048]{1,0:T(8,128)(2,1)S(1)}, bf16[128,2048]{1,0:T(8,128)(2,1)S(1)}, u32[]{:S(2)}, u32[]{:S(2)}) %collective-permute-start.2) | collective-permute-done | bytes 524320 | tf_op jit(solution)/shard_map/ppermute | solution.py:66
  46.3 2.8 collective-permute-done.3
  52.0 4.8 %collective-permute-done.4 = bf16[128,1024]{1,0:T(8,128)(2,1)S(1)} collective-permute-done((bf16[128,1024]{1,0:T(8,128)(2,1)S(1)}, bf16[128,1024]{1,0:T(8,128)(2,1)S(1)}, u32[]{:S(2)}, u32[]{:S(2)}) %collective-permute-start.4) | collective-permute-done | bytes 262176 | tf_op jit(solution)/shard_map/ppermute | solution.py:66
  57.1 54.3 %shard_map.203 = (bf16[16,128,1024]{2,1,0:T(8,128)(2,1)S(1)}, bf16[16,128,128]{2,1,0:T(8,128)(2,1)S(1)}) custom-call(bf16[128,1024]{1,0:T(8,128)(2,1)S(1)} %multiply_convert_fusion.5.refs_0_, bf16[128,128]{1,0:T(8,128)(2,1)S(1)} %pad_convert_fusion.refs_1_), custom_call_target="tpu_custom_call" | custom-call | tf_op jit(solution)/shard_map/pallas_call | solution.py:328
  114.5 3.6 fusion.88
  118.8 7.0 %fusion.8 = f32[2048,1024]{0,1:T(8,128)} fusion(bf16[2048,1024]{1,0:T(8,128)(2,1)S(1)} %bitcast.121, bf16[1,1024,1024]{2,1,0:T(8,128)(2,1)S(1)} %copy-done), kind=kOutput, calls=%fused_computation.24 | convolution fusion | flops 4294967296 | bytes 14680064 | tf_op jit(solution)/shard_map/dot_general | solution.py:49
  125.8 8.1 %multiply_convert_fusion.1 = (bf16[2048,512]{0,1:T(8,128)(2,1)S(1)}, bf16[2048,512]{0,1:T(8,128)(2,1)S(1)}, bf16[2048,512]{0,1:T(8,128)(2,1)S(1)}) fusion(f32[2048,1024]{0,1:T(8,128)} %fusion.8, bf16[1,512,1024]{2,1,0:T(8,128)(2,1)} %param.21, bf16[2048,1024]{1,0:T(8,128)(2,1)} %all-gather.2.cloned.1.call-done, f32[2048]{0:T(1024)S(1)} %broadcast_multiply_fusion), kind=kOutput, calls=%fused_computation.12 | convolution fusion | flops 2170552320 | bytes 19931136 | tf_op jit(solution)/shard_map/dot_general | solution.py:59
  134.0 7.4 %fusion.6 = f32[1024,1024]{1,0:T(8,128)} fusion(bf16[2048,1024]{1,0:T(8,128)(2,1)S(1)} %bitcast.122, bf16[2048,512]{0,1:T(8,128)(2,1)S(1)} %get-tuple-element.22, bf16[2048,512]{0,1:T(8,128)(2,1)S(1)} %get-tuple-element.21), kind=kOutput, calls=%fused_computation.20 | convolution fusion | flops 4303355904 | bytes 12582912 | tf_op jit(solution)/shard_map/dot_general | solution.py:53
  141.4 6.2 %convolution_convert_fusion.1 = bf16[2048,1024]{1,0:T(8,128)(2,1)} fusion(bf16[2048,512]{0,1:T(8,128)(2,1)S(1)} %get-tuple-element.22, bf16[2048,512]{0,1:T(8,128)(2,1)S(1)} %get-tuple-element.21, bf16[1,1024,1024]{2,1,0:T(8,128)(2,1)S(1)} %copy-done), kind=kOutput, calls=%fused_computation.16 | convolution fusion | flops 4305453056 | bytes 10485760 | tf_op jit(solution)/shard_map/dot_general | solution.py:59
  147.6 5.3 %fusion.2 = (f32[2048]{0:T(1024)}, bf16[2048,1024]{1,0:T(8,128)(2,1)}) fusion(bf16[2048,1024]{1,0:T(8,128)(2,1)S(1)} %copy-done.44, f32[2048]{0:T(1024)S(1)} %select_reduce_fusion, bf16[2048,512]{0,1:T(8,128)(2,1)S(1)} %get-tuple-element.23, bf16[1,512,1024]{2,1,0:T(8,128)(2,1)S(1)} %copy-done.45), kind=kOutput, calls=%fused_computation.6 | convolution fusion | flops 2164258816 | bytes 11550720 | tf_op jit(solution)/shard_map/dot_general | solution.py:49
  152.9 3.4 all-to-all-start
  156.4 6.7 %fusion.10 = f32[512,1024]{1,0:T(8,128)} fusion(bf16[2048,512]{0,1:T(8,128)(2,1)} %copy-done.48, bf16[2048,1024]{1,0:T(8,128)(2,1)} %all-gather.2.cloned.1.call-done, f32[2048]{0:T(1024)S(1)} %broadcast_multiply_fusion), kind=kOutput, calls=%fused_computation.28 | convolution fusion | flops 2153775104 | bytes 8396800 | tf_op jit(solution)/shard_map/dot_general | solution.py:53
  163.1 36.0 %shard_map.204 = f32[128,1024]{1,0:T(8,128)S(1)} custom-call(bf16[16,128,1024]{2,1,0:T(8,128)(2,1)S(1)} %bitcast.123), custom_call_target="tpu_custom_call" | custom-call | tf_op jit(solution)/shard_map/pallas_call | solution.py:348
  203.5 2.7 dynamic-slice_convert_fusion
  212.2 31.7 %collective-permute-done.7 = bf16[128,512]{1,0:T(8,128)(2,1)S(1)} collective-permute-done((bf16[128,512]{1,0:T(8,128)(2,1)S(1)}, bf16[128,512]{1,0:T(8,128)(2,1)S(1)}, u32[]{:S(2)}, u32[]{:S(2)}) %collective-permute-start.7) | collective-permute-done | bytes 131104 | tf_op jit(solution)/shard_map/ppermute | solution.py:66
  251.8 2.3 add_bitcast_fusion.1
  254.1 6.7 %collective-permute-done.8 = bf16[128,2048]{0,1:T(8,128)(2,1)S(1)} collective-permute-done((bf16[128,2048]{0,1:T(8,128)(2,1)S(1)}, bf16[128,2048]{0,1:T(8,128)(2,1)S(1)}, u32[]{:S(2)}, u32[]{:S(2)}) %collective-permute-start.8) | collective-permute-done | bytes 524320 | tf_op jit(solution)/shard_map/ppermute | solution.py:66
  264.9 2.1 fusion.5
  267.0 68.2 %shard_map.205 = bf16[16,32,3200]{2,1,0:T(8,128)(2,1)S(1)} custom-call(bf16[16,32,3200]{2,1,0:T(8,128)(2,1)} %bitcast.125), custom_call_target="tpu_custom_call" | custom-call | tf_op jit(solution)/shard_map/pallas_call | solution.py:371
  335.9 2.8 copy-done.6
  341.8 3.0 fusion.84
  344.9 5.0 %fusion.83 = (f32[512,1024]{1,0:T(8,128)}, f32[512,1024]{1,0:T(8,128)}) fusion(f32[512,3200]{1,0:T(8,128)} %copy-done.6), kind=kLoop, calls=%fused_computation.188 | loop fusion | bytes 8388608 | tf_op jit(solution)/shard_map/slice | solution.py:554
  349.8 3.0 add_bitcast_fusion
  353.5 2.4 fusion.28
  (211 shorter events, 61.4 us)
Async XLA Ops:
  7.2 111.7 %copy-start = (bf16[1,1024,1024]{2,1,0:T(8,128)(2,1)S(1)}, bf16[1,1024,1024]{2,1,0:T(8,128)(2,1)}, u32[]{:S(2)}) copy-start(bf16[1,1024,1024]{2,1,0:T(8,128)(2,1)} %param.20) | copy-start | bytes 6291460
  7.2 118.6 %all-gather.2.cloned.1.call-start = ((), (), s32[]{:S(2)}) async-start(), calls=%async_computation.3 | async-start | bytes 4456448 | tf_op jit(solution)/shard_map/all_gather | solution.py:412
  8.5 11.0 %collective-permute-start = (bf16[128,512]{1,0:T(8,128)(2,1)S(1)}, bf16[128,512]{1,0:T(8,128)(2,1)S(1)}, u32[]{:S(2)}, u32[]{:S(2)}) collective-permute-start(bf16[128,512]{1,0:T(8,128)(2,1)S(1)} %get-tuple-element.49), channel_id=1, source_target_pairs={{0,1},{1,0},{2,3},{3,2},{4,5},{5,4},{6,7},{7,6},{8,9},{9,8},{10,11... | collective-permute-start | bytes 393224 | tf_op jit(solution)/shard_map/ppermute | solution.py:66
  11.4 7.4 %collective-permute-start.1 = (f32[128,1]{0,1:T(1,128)}, f32[128,1]{0,1:T(1,128)}, u32[]{:S(2)}, u32[]{:S(2)}) collective-permute-start(f32[128,1]{0,1:T(1,128)} %get-tuple-element.51), channel_id=1, source_target_pairs={{0,1},{1,0},{2,3},{3,2},{4,5},{5,4},{6,7},{7,6},{8,9},{9,8},{10,11... | collective-permute-start | bytes 1544 | tf_op jit(solution)/shard_map/ppermute | solution.py:66
  14.2 31.3 %collective-permute-start.5 = (bf16[512,17]{0,1:T(8,128)(2,1)}, bf16[512,17]{0,1:T(8,128)(2,1)}, u32[]{:S(2)}, u32[]{:S(2)}) collective-permute-start(bf16[512,17]{0,1:T(8,128)(2,1)} %constant_dynamic-update-slice_fusion), channel_id=1, source_target_pairs={{0,1},{1,0},{2,3},{3,2},{4,5},{5,4},{6,7},{7,6},{8,9},{9,8},{10,11... | collective-permute-start | bytes 52232 | tf_op jit(solution)/shard_map/ppermute | solution.py:66
  23.9 12.0 %collective-permute-start.2 = (bf16[128,2048]{1,0:T(8,128)(2,1)S(1)}, bf16[128,2048]{1,0:T(8,128)(2,1)S(1)}, u32[]{:S(2)}, u32[]{:S(2)}) collective-permute-start(bf16[128,2048]{1,0:T(8,128)(2,1)S(1)} %slice.184), channel_id=1, source_target_pairs={{0,1},{1,0},{2,3},{3,2},{4,5},{5,4},{6,7},{7,6},{8,9},{9,8},{10,11... | collective-permute-start | bytes 1572872 | tf_op jit(solution)/shard_map/ppermute | solution.py:66
  41.9 72.3 %copy-start.35 = (pred[128,16]{0,1:T(8,128)(4,1)S(1)}, pred[128,16]{0,1:T(8,128)(4,1)}, u32[]{:S(2)}) copy-start(pred[128,16]{0,1:T(8,128)(4,1)} %fusion.50) | copy-start | bytes 6148
  44.7 4.4 %collective-permute-start.3 = (bf16[128,512]{0,1:T(8,128)(2,1)}, bf16[128,512]{0,1:T(8,128)(2,1)}, u32[]{:S(2)}, u32[]{:S(2)}) collective-permute-start(bf16[128,512]{0,1:T(8,128)(2,1)} %get-tuple-element.47), channel_id=1, source_target_pairs={{0,1},{1,0},{2,3},{3,2},{4,5},{5,4},{6,7},{7,6},{8,9},{9,8},{10,11... | collective-permute-start | bytes 393224 | tf_op jit(solution)/shard_map/ppermute | solution.py:66
  51.0 5.7 %collective-permute-start.4 = (bf16[128,1024]{1,0:T(8,128)(2,1)S(1)}, bf16[128,1024]{1,0:T(8,128)(2,1)S(1)}, u32[]{:S(2)}, u32[]{:S(2)}) collective-permute-start(bf16[128,1024]{1,0:T(8,128)(2,1)S(1)} %slice.185), channel_id=1, source_target_pairs={{0,1},{1,0},{2,3},{3,2},{4,5},{5,4},{6,7},{7,6},{8,9},{9,8},{10,11... | collective-permute-start | bytes 786440 | tf_op jit(solution)/shard_map/ppermute | solution.py:66
  56.9 56.5 %copy-start.38 = (f32[128]{0:T(128)}, f32[128]{0:T(128)S(1)}, u32[]{:S(2)}) copy-start(f32[128]{0:T(128)S(1)} %add_rsqrt_fusion) | copy-start | bytes 1540
  152.9 46.2 %all-to-all-start = ((f32[16,1,128]{2,1,0:T(1,128)}), f32[16,1,128]{2,1,0:T(1,128)S(1)}, u32[]{:S(2)}, u32[]{:S(2)}) async-start(f32[16,1,128]{2,1,0:T(1,128)} %bitcast.22), calls=%async_computation.1 | async-start | bytes 16384 | tf_op jit(solution)/shard_map/all_to_all | solution.py:464
  156.3 197.2 %reduce-scatter.2.cloned.1.call-start = ((), (), s32[]{:S(2)}) async-start(), calls=%async_computation.2 | async-start | bytes 4456448 | tf_op jit(solution)/shard_map/reduce_scatter | solution.py:458
  163.1 36.5 %copy-start.12 = (bf16[128,1024]{1,0:T(8,128)(2,1)S(1)}, bf16[128,1024]{1,0:T(8,128)(2,1)}, u32[]{:S(2)}) copy-start(bf16[128,1024]{1,0:T(8,128)(2,1)} %param.23) | copy-start | bytes 786436
  199.8 7.5 %collective-permute-start.6 = (bf16[128,1024]{1,0:T(8,128)(2,1)S(1)}, bf16[128,1024]{1,0:T(8,128)(2,1)S(1)}, u32[]{:S(2)}, u32[]{:S(2)}) collective-permute-start(bf16[128,1024]{1,0:T(8,128)(2,1)S(1)} %multiply_convert_fusion.4), channel_id=1, source_target_pairs={{0,1},{1,0},{2,3},{3,2},{4,5},{5,4},{6,7},{7,6},{8,9},{9,8},{10,11... | collective-permute-start | bytes 786440 | tf_op jit(solution)/shard_map/ppermute | solution.py:66
  202.3 49.5 %collective-permute-start.12 = (bf16[512,512]{1,0:T(8,128)(2,1)}, bf16[512,512]{1,0:T(8,128)(2,1)}, u32[]{:S(2)}, u32[]{:S(2)}) collective-permute-start(bf16[512,512]{1,0:T(8,128)(2,1)} %dynamic-slice_convert_fusion.1), channel_id=1, source_target_pairs={{0,1},{1,0},{2,3},{3,2},{4,5},{5,4},{6,7},{7,6},{8,9},{9,8},{10,11... | collective-permute-start | bytes 1572872 | tf_op jit(solution)/shard_map/ppermute | solution.py:66
  206.1 37.9 %copy-start.8 = (f32[8,2,128,128]{2,3,1,0:T(8,128)S(1)}, f32[8,2,128,128]{2,3,1,0:T(8,128)}, u32[]{:S(2)}) copy-start(f32[8,2,128,128]{2,3,1,0:T(8,128)} %copy-done.7) | copy-start | bytes 3145732
  206.1 37.9 %copy-start.15 = (bf16[128,512]{0,1:T(8,128)(2,1)S(1)}, bf16[128,512]{0,1:T(8,128)(2,1)}, u32[]{:S(2)}) copy-start(bf16[128,512]{0,1:T(8,128)(2,1)} %copy.84) | copy-start | bytes 393220
  206.1 37.9 %copy-start.36 = (f32[8,2,128]{2,1,0:T(2,128)S(1)}, f32[8,2,128]{2,1,0:T(2,128)}, u32[]{:S(2)}) copy-start(f32[8,2,128]{2,1,0:T(2,128)} %multiply_divide_fusion) | copy-start | bytes 24580
  206.2 143.7 %collective-permute-start.11 = (bf16[1024,512]{1,0:T(8,128)(2,1)}, bf16[1024,512]{1,0:T(8,128)(2,1)}, u32[]{:S(2)}, u32[]{:S(2)}) collective-permute-start(bf16[1024,512]{1,0:T(8,128)(2,1)} %dynamic-slice_convert_fusion), channel_id=1, source_target_pairs={{0,1},{1,0},{2,3},{3,2},{4,5},{5,4},{6,7},{7,6},{8,9},{9,8},{10,11... | collective-permute-start | bytes 3145736 | tf_op jit(solution)/shard_map/ppermute | solution.py:66
  206.5 38.0 %copy-start.34 = (pred[128,128]{0,1:T(8,128)(4,1)S(1)}, pred[128,128]{0,1:T(8,128)(4,1)}, u32[]{:S(2)}) copy-start(pred[128,128]{0,1:T(8,128)(4,1)} %iota_compare_fusion.2) | copy-start | bytes 49156
  209.8 34.2 %collective-permute-start.7 = (bf16[128,512]{1,0:T(8,128)(2,1)S(1)}, bf16[128,512]{1,0:T(8,128)(2,1)S(1)}, u32[]{:S(2)}, u32[]{:S(2)}) collective-permute-start(bf16[128,512]{1,0:T(8,128)(2,1)S(1)} %get-tuple-element.45), channel_id=1, source_target_pairs={{0,1},{1,0},{2,3},{3,2},{4,5},{5,4},{6,7},{7,6},{8,9},{9,8},{10,11... | collective-permute-start | bytes 393224 | tf_op jit(solution)/shard_map/ppermute | solution.py:66
  211.0 38.5 %collective-permute-start.10 = (f32[512,17]{0,1:T(8,128)}, f32[512,17]{0,1:T(8,128)}, u32[]{:S(2)}, u32[]{:S(2)}) collective-permute-start(f32[512,17]{0,1:T(8,128)} %fusion.51), channel_id=1, source_target_pairs={{0,1},{1,0},{2,3},{3,2},{4,5},{5,4},{6,7},{7,6},{8,9},{9,8},{10,11... | collective-permute-start | bytes 104456 | tf_op jit(solution)/shard_map/ppermute | solution.py:66
  249.1 11.7 %collective-permute-start.8 = (bf16[128,2048]{0,1:T(8,128)(2,1)S(1)}, bf16[128,2048]{0,1:T(8,128)(2,1)S(1)}, u32[]{:S(2)}, u32[]{:S(2)}) collective-permute-start(bf16[128,2048]{0,1:T(8,128)(2,1)S(1)} %pad_maximum_fusion.6), channel_id=1, source_target_pairs={{0,1},{1,0},{2,3},{3,2},{4,5},{5,4},{6,7},{7,6},{8,9},{9,8},{10,11... | collective-permute-start | bytes 1572872 | tf_op jit(solution)/shard_map/ppermute | solution.py:66
  339.4 13.4 %collective-permute-start.9 = (bf16[128,512]{1,0:T(8,128)(2,1)S(1)}, bf16[128,512]{1,0:T(8,128)(2,1)S(1)}, u32[]{:S(2)}, u32[]{:S(2)}) collective-permute-start(bf16[128,512]{1,0:T(8,128)(2,1)S(1)} %get-tuple-element.42), channel_id=1, source_target_pairs={{0,1},{1,0},{2,3},{3,2},{4,5},{5,4},{6,7},{7,6},{8,9},{9,8},{10,11... | collective-permute-start | bytes 393224 | tf_op jit(solution)/shard_map/ppermute | solution.py:66
  (41 other events, 349.4 us)
Sparse Core Ops, SparseCore 0:
  10.2 52.1 all-gather.1
  206.6 71.1 reduce-scatter.1

commit v3 on v2

--- a/solution.py
+++ b/solution.py
@@ -455,22 +455,32 @@
     sig = jax.nn.sigmoid(g)
     hid = (g * sig * u).astype(BF16)
     y = product(hid, w_dn).astype(BF16).astype(F32)
-    mixture = lax.psum_scatter(
-        (gate * y).astype(BF16), "expert", scatter_dimension=0, tiled=True
-    )
     og_scaled = RESIDUAL * og_all.astype(F32)
     dy = (gate * og_scaled).astype(BF16)
-    gate_grad_col = jnp.sum(y * og_scaled, axis=-1).reshape(experts, tokens)
-    gate_grad = lax.all_to_all(gate_grad_col, "expert", split_axis=0, concat_axis=0, tiled=True).T
+    gate_grad_col = jnp.sum(y * og_scaled, axis=-1, keepdims=True)
+    high = gate_grad_col.astype(BF16)
+    low = (gate_grad_col - high.astype(F32)).astype(BF16)
+    extra = jnp.concatenate([jnp.where(mine, high, 0), jnp.where(mine, low, 0)], axis=1)
+    extra = jnp.pad(extra, ((0, 0), (0, -extra.shape[1] % 128)))
+    dy, gated = lax.optimization_barrier((dy, (gate * y).astype(BF16)))
+    mixture = lax.psum_scatter(gated, "expert", scatter_dimension=0, tiled=True)
     dhid = right_transposed(dy, w_dn)
     dgu = jnp.concatenate(
         [dhid * u * sig * (1.0 + g * (1.0 - sig)), dhid * g * sig], axis=1
     ).astype(BF16)
-    token_grad = scatter_expert(right_transposed(dgu, w_gu).astype(BF16), 2)
-    down_sum = sum_pieces(left_product(hid, dy), 1)
-    gate_up_sum = sum_pieces(left_product(x_all, dgu), 1)
-
-    output = (middle + RESIDUAL * mixture.astype(F32)).astype(BF16)
+    row_grad = right_transposed(dgu, w_gu).astype(BF16)
+    down_local, gate_up_local = left_product(hid, dy), left_product(x_all, dgu)
+    row_grad, down_local, gate_up_local = lax.optimization_barrier(
+        (row_grad, down_local, gate_up_local)
+    )
+    down_sum, gate_up_sum = sum_pieces(down_local, 1), sum_pieces(gate_up_local, 1)
+    scattered = scatter_expert(jnp.concatenate([row_grad, extra], axis=1), 2)
+    token_grad = scattered[:, :model_width]
+    gate_grad = (
+        scattered[:, model_width : model_width + experts]
+        + scattered[:, model_width + experts : model_width + 2 * experts]
+    )
+
     upstream = out_grad.astype(F32)
     gates = jax.nn.softmax(
         jnp.where(mask, product(xn_two, router_w), NEGATIVE), axis=-1
@@ -488,6 +498,9 @@
     )
     branch_low = (RESIDUAL * middle_grad).astype(BF16)
     router_local = left_product(xn_two, logit_grad)
+    branch_low, down_sum, gate_up_sum = lax.optimization_barrier(
+        (branch_low, down_sum, gate_up_sum)
+    )
     branch_all = rows_of_all(branch_low)
     attended_grad = columns_home(right_transposed(branch_all, w_out).astype(BF16))
     output_local = left_product(attended_cols, branch_all).astype(BF16)
@@ -495,6 +508,7 @@
         jnp.concatenate([router_local, gain_two_grad[:, None]], axis=1), 0, F32
     )
 
+    attended_grad, mixture = lax.optimization_barrier((attended_grad, mixture))
     attended_grad = attended_grad.reshape(tokens, kv_heads, groups, HEAD_DIM)
     value_grad = jnp.einsum(
         "kgts,tkgd->skd", probs_low, attended_grad, preferred_element_type=F32
@@ -520,6 +534,7 @@
         ],
         axis=1,
     )
+    output = (middle + RESIDUAL * mixture.astype(F32)).astype(BF16)
     qkv_all = rows_of_all(qkv_grad)
     xn_one_grad = (
         right_transposed(qkv_all[:, :q_width], w_query)

time: 364 us -> 372 us (1.022)
  waiting for transfers between devices: 57.7 us -> 31.3 us
  Pallas kernels: 159 us -> 184 us
  other arithmetic: 23.6 us -> 31.7 us
    ppermute x13, waiting for transfers between devices: 57.7 us -> 31.2 us  [shift(): lax.ppermute(values, 'shard', [(i, (i + step) % n) for i in range(n)])]
    pallas_call x1, Pallas kernels: 36 us -> 55.8 us  [scatter_expert(): pl.pallas_call(partial(scatter_kernel, n), out_shape=jax.ShapeDtypeStruct...]
    dot_general x5, matrix products: 17.4 us -> 10.6 us  [left_product(): lax.dot_general(left_rows, right_rows, (((0,), (0,)), ((), ())), preferre...]
    add x0 -> x2, other arithmetic: none -> 5.37 us  [sum_pieces(): total + shift(piece(values, me + d, axis).astype(sent), d).astype(F32)]
    broadcast_in_dim x2 -> x0, other arithmetic: 5.3 us -> none  [the longest x1 2.98 us: shards(): gate_up_sum[None]]
    dot_general x7, matrix products: 18.3 us -> 22.4 us  [right_transposed(): lax.dot_general(left_rows, weight, (((1,), (1,)), ((), ())), preferred_el...]
    pallas_call x1, Pallas kernels: 54.3 us -> 58.3 us  [gather_expert(): pl.pallas_call(partial(gather_kernel, n, count), out_shape=[jax.ShapeDtyp...]
    unnamed x101 -> x125, local copies, waits for them, and re-layouts: 9.88 us -> 13.4 us
  transfers between devices with their start and end apart: 16 -> 15, of which waited for: 6 -> 6; matrix products, arithmetic and copies ran while one was open for 23% -> 21% of each run, Pallas kernels for 44% -> 31%
where the time goes in v3:
time: 372 us; the launch traced here: 367 us
  Pallas kernels  184 us (49%)
  matrix products  62.1 us (17%)
  local copies, waits for them, and re-layouts  31.8 us (9%)
  other arithmetic  31.7 us (9%)
  waiting for transfers between devices  31.3 us (8%)
  between operations  15.5 us (4%)
  starting transfers between devices  10.8 us (3%)
    pallas_call x1, Pallas kernels, sum_expert(): pl.pallas_call(partial(sum_kernel, n), out_shape=jax.ShapeDtypeStruct((n,...  69.6 us
    pallas_call x1, Pallas kernels, gather_expert(): pl.pallas_call(partial(gather_kernel, n, count), out_shape=[jax.ShapeDtyp...  58.3 us
    pallas_call x1, Pallas kernels, scatter_expert(): pl.pallas_call(partial(scatter_kernel, n), out_shape=jax.ShapeDtypeStruct...  55.8 us
    ppermute x13, waiting for transfers between devices, shift(): lax.ppermute(values, 'shard', [(i, (i + step) % n) for i in range(n)])  31.2 us
    dot_general x8, matrix products, product(): return jnp.dot(left, right, preferred_element_type=F32)  22.7 us
    dot_general x7, matrix products, right_transposed(): lax.dot_general(left_rows, weight, (((1,), (1,)), ((), ())), preferred_el...  22.4 us
    unnamed x125, local copies, waits for them, and re-layouts  13.4 us
    ppermute x13, starting transfers between devices, shift(): lax.ppermute(values, 'shard', [(i, (i + step) % n) for i in range(n)])  10.7 us
  transfers between devices with their start and end apart: 15, of which 6 were waited for; matrix products, arithmetic and copies ran while one was open for 21% of the time, Pallas kernels for 31%

profile of v3, /device:TPU:9, one launch (start us, length us, event | category | flops | bytes accessed | tf_op | source)
XLA Modules:
  0.0 367.0 jit_solution(5475927462565623703)
XLA Ops:
  22.2 9.7 %collective-permute-done.2 = bf16[128,2048]{1,0:T(8,128)(2,1)S(1)} collective-permute-done((bf16[128,2048]{1,0:T(8,128)(2,1)S(1)}, bf16[128,2048]{1,0:T(8,128)(2,1)S(1)}, u32[]{:S(2)}, u32[]{:S(2)}) %collective-permute-start.2) | collective-permute-done | bytes 524320 | tf_op jit(solution)/shard_map/ppermute | solution.py:66
  37.1 2.2 fusion.83
  43.5 2.6 collective-permute-done.3
  49.1 4.6 %collective-permute-done.4 = bf16[128,1024]{1,0:T(8,128)(2,1)S(1)} collective-permute-done((bf16[128,1024]{1,0:T(8,128)(2,1)S(1)}, bf16[128,1024]{1,0:T(8,128)(2,1)S(1)}, u32[]{:S(2)}, u32[]{:S(2)}) %collective-permute-start.4) | collective-permute-done | bytes 262176 | tf_op jit(solution)/shard_map/ppermute | solution.py:66
  54.5 58.3 %shard_map.203 = (bf16[16,128,1024]{2,1,0:T(8,128)(2,1)S(1)}, bf16[16,128,128]{2,1,0:T(8,128)(2,1)S(1)}) custom-call(bf16[128,1024]{1,0:T(8,128)(2,1)S(1)} %multiply_convert_fusion.5.refs_0_, bf16[128,128]{1,0:T(8,128)(2,1)S(1)} %pad_convert_fusion.refs_1_), custom_call_target="tpu_custom_call" | custom-call | tf_op jit(solution)/shard_map/pallas_call | solution.py:328
  117.0 3.4 fusion.84
  120.6 4.9 %fusion.10 = f32[2048,1024]{0,1:T(8,128)S(1)} fusion(bf16[2048,1024]{1,0:T(8,128)(2,1)S(1)} %bitcast.119, bf16[1,1024,1024]{2,1,0:T(8,128)(2,1)S(1)} %copy-done), kind=kOutput, calls=%fused_computation.27 | convolution fusion | flops 4294967296 | bytes 14680064 | tf_op jit(solution)/shard_map/dot_general | solution.py:49
  125.5 3.3 copy-done.8
  128.8 2.6 multiply_convert_fusion.2
  131.3 8.2 %fusion.3 = (bf16[2048,1024]{1,0:T(8,128)(2,1)}, f32[2048]{0:T(1024)S(1)}, bf16[2048,1024]{1,0:T(8,128)(2,1)}) fusion(f32[2048]{0:T(1024)S(1)} %select_reduce_fusion, bf16[2048,1024]{1,0:T(8,128)(2,1)} %all-gather.2.cloned.1.call-done, f32[2048]{0:T(1024)S(1)} %broadcast_multiply_fusion, bf16[2048,512]{0,1:T(8,128)(2,1)} %multiply_convert_fusion.2, ...), kind=kOutput, calls=%fused_computation.8 | convolution fusion | flops 2168453120 | bytes 15753216 | tf_op jit(solution)/shard_map/dot_general | solution.py:49
  139.5 10.5 %multiply_convert_fusion.1 = (bf16[2048,512]{0,1:T(8,128)(2,1)}, bf16[2048,512]{0,1:T(8,128)(2,1)}) fusion(f32[2048,1024]{0,1:T(8,128)} %copy-done.8, bf16[2048,1024]{1,0:T(8,128)(2,1)} %get-tuple-element.25, bf16[1,512,1024]{2,1,0:T(8,128)(2,1)} %param.21), kind=kOutput, calls=%fused_computation.15 | convolution fusion | flops 2161115136 | bytes 17825792 | tf_op jit(solution)/shard_map/dot_general | solution.py:59
  150.0 3.7 %fusion.86 = f32[512,1024]{1,0:T(8,128)} fusion(bf16[2048,512]{0,1:T(8,128)(2,1)S(1)} %copy-done.19, bf16[2048,1024]{1,0:T(8,128)(2,1)S(1)} %copy-done.57), kind=kOutput, calls=%fused_computation.199 | convolution fusion | flops 2147483648 | bytes 8388608 | tf_op jit(solution)/shard_map/dot_general | solution.py:53
  153.8 8.9 %convolution_convert_fusion.1 = bf16[2048,1024]{1,0:T(8,128)(2,1)} fusion(bf16[2048,512]{0,1:T(8,128)(2,1)} %get-tuple-element.44, bf16[2048,512]{0,1:T(8,128)(2,1)} %get-tuple-element.43, bf16[1,1024,1024]{2,1,0:T(8,128)(2,1)S(1)} %copy-done), kind=kOutput, calls=%fused_computation.19 | convolution fusion | flops 4305453056 | bytes 10485760 | tf_op jit(solution)/shard_map/dot_general | solution.py:59
  162.7 4.5 %fusion.8 = f32[1024,1024]{1,0:T(8,128)S(1)} fusion(bf16[2048,1024]{1,0:T(8,128)(2,1)S(1)} %bitcast.120, bf16[2048,512]{0,1:T(8,128)(2,1)S(1)} %copy-done.59, bf16[2048,512]{0,1:T(8,128)(2,1)S(1)} %copy-done.58), kind=kOutput, calls=%fused_computation.23 | convolution fusion | flops 4303355904 | bytes 12582912 | tf_op jit(solution)/shard_map/dot_general | solution.py:53
  171.5 2.1 dynamic-slice_convert_fusion.1
  174.4 2.7 fusion.6
  177.1 55.8 %shard_map.204 = f32[128,1152]{1,0:T(8,128)S(1)} custom-call(bf16[16,128,1152]{2,1,0:T(8,128)(2,1)S(1)} %bitcast.117), custom_call_target="tpu_custom_call" | custom-call | tf_op jit(solution)/shard_map/pallas_call | solution.py:348
  234.6 2.3 convert_add_fusion.1
  236.9 3.1 convert_add_fusion
  242.0 5.7 %collective-permute-done.8 = bf16[128,1024]{1,0:T(8,128)(2,1)S(1)} collective-permute-done((bf16[128,1024]{1,0:T(8,128)(2,1)S(1)}, bf16[128,1024]{1,0:T(8,128)(2,1)S(1)}, u32[]{:S(2)}, u32[]{:S(2)}) %collective-permute-start.8) | collective-permute-done | bytes 262176 | tf_op jit(solution)/shard_map/ppermute | solution.py:66
  261.4 7.1 %collective-permute-done.10 = bf16[128,2048]{0,1:T(8,128)(2,1)S(1)} collective-permute-done((bf16[128,2048]{0,1:T(8,128)(2,1)S(1)}, bf16[128,2048]{0,1:T(8,128)(2,1)S(1)}, u32[]{:S(2)}, u32[]{:S(2)}) %collective-permute-start.10) | collective-permute-done | bytes 524320 | tf_op jit(solution)/shard_map/ppermute | solution.py:66
  275.2 69.6 %shard_map.205 = bf16[16,32,3200]{2,1,0:T(8,128)(2,1)S(1)} custom-call(bf16[16,32,3200]{2,1,0:T(8,128)(2,1)} %bitcast.122), custom_call_target="tpu_custom_call" | custom-call | tf_op jit(solution)/shard_map/pallas_call | solution.py:371
  345.4 3.0 fusion.79
  357.6 2.2 fusion.27
  (239 shorter events, 70.5 us)
Async XLA Ops:
  7.2 113.4 %copy-start = (bf16[1,1024,1024]{2,1,0:T(8,128)(2,1)S(1)}, bf16[1,1024,1024]{2,1,0:T(8,128)(2,1)}, u32[]{:S(2)}) copy-start(bf16[1,1024,1024]{2,1,0:T(8,128)(2,1)} %param.20) | copy-start | bytes 6291460
  7.2 124.1 %all-gather.2.cloned.1.call-start = ((), (), s32[]{:S(2)}) async-start(), calls=%async_computation.1 | async-start | bytes 4456448 | tf_op jit(solution)/shard_map/all_gather | solution.py:412
  8.5 7.8 %collective-permute-start = (bf16[128,512]{1,0:T(8,128)(2,1)S(1)}, bf16[128,512]{1,0:T(8,128)(2,1)S(1)}, u32[]{:S(2)}, u32[]{:S(2)}) collective-permute-start(bf16[128,512]{1,0:T(8,128)(2,1)S(1)} %get-tuple-element.71), channel_id=1, source_target_pairs={{0,1},{1,0},{2,3},{3,2},{4,5},{5,4},{6,7},{7,6},{8,9},{9,8},{10,11... | collective-permute-start | bytes 393224 | tf_op jit(solution)/shard_map/ppermute | solution.py:66
  11.4 4.8 %collective-permute-start.1 = (f32[128,1]{0,1:T(1,128)S(1)}, f32[128,1]{0,1:T(1,128)S(1)}, u32[]{:S(2)}, u32[]{:S(2)}) collective-permute-start(f32[128,1]{0,1:T(1,128)S(1)} %get-tuple-element.73), channel_id=1, source_target_pairs={{0,1},{1,0},{2,3},{3,2},{4,5},{5,4},{6,7},{7,6},{8,9},{9,8},{10,11... | collective-permute-start | bytes 1544 | tf_op jit(solution)/shard_map/ppermute | solution.py:66
  14.2 34.0 %collective-permute-start.5 = (bf16[512,17]{0,1:T(8,128)(2,1)}, bf16[512,17]{0,1:T(8,128)(2,1)}, u32[]{:S(2)}, u32[]{:S(2)}) collective-permute-start(bf16[512,17]{0,1:T(8,128)(2,1)} %constant_dynamic-update-slice_fusion), channel_id=1, source_target_pairs={{0,1},{1,0},{2,3},{3,2},{4,5},{5,4},{6,7},{7,6},{8,9},{9,8},{10,11... | collective-permute-start | bytes 52232 | tf_op jit(solution)/shard_map/ppermute | solution.py:66
  15.5 236.7 %reduce-scatter.2.cloned.1.call-start = ((), (), s32[]{:S(2)}) async-start(), calls=%async_computation.2 | async-start | bytes 4456448 | tf_op jit(solution)/shard_map/reduce_scatter | solution.py:466
  19.9 12.0 %collective-permute-start.2 = (bf16[128,2048]{1,0:T(8,128)(2,1)S(1)}, bf16[128,2048]{1,0:T(8,128)(2,1)S(1)}, u32[]{:S(2)}, u32[]{:S(2)}) collective-permute-start(bf16[128,2048]{1,0:T(8,128)(2,1)S(1)} %slice.207), channel_id=1, source_target_pairs={{0,1},{1,0},{2,3},{3,2},{4,5},{5,4},{6,7},{7,6},{8,9},{9,8},{10,11... | collective-permute-start | bytes 1572872 | tf_op jit(solution)/shard_map/ppermute | solution.py:66
  37.1 16.6 %copy-start.9 = (bf16[128,1024]{1,0:T(8,128)(2,1)S(1)}, bf16[128,1024]{1,0:T(8,128)(2,1)}, u32[]{:S(2)}) copy-start(bf16[128,1024]{1,0:T(8,128)(2,1)} %param.12) | copy-start | bytes 786436
  41.9 4.3 %collective-permute-start.3 = (bf16[128,512]{0,1:T(8,128)(2,1)}, bf16[128,512]{0,1:T(8,128)(2,1)}, u32[]{:S(2)}, u32[]{:S(2)}) collective-permute-start(bf16[128,512]{0,1:T(8,128)(2,1)} %get-tuple-element.69), channel_id=1, source_target_pairs={{0,1},{1,0},{2,3},{3,2},{4,5},{5,4},{6,7},{7,6},{8,9},{9,8},{10,11... | collective-permute-start | bytes 393224 | tf_op jit(solution)/shard_map/ppermute | solution.py:66
  48.0 5.7 %collective-permute-start.4 = (bf16[128,1024]{1,0:T(8,128)(2,1)S(1)}, bf16[128,1024]{1,0:T(8,128)(2,1)S(1)}, u32[]{:S(2)}, u32[]{:S(2)}) collective-permute-start(bf16[128,1024]{1,0:T(8,128)(2,1)S(1)} %slice.208), channel_id=1, source_target_pairs={{0,1},{1,0},{2,3},{3,2},{4,5},{5,4},{6,7},{7,6},{8,9},{9,8},{10,11... | collective-permute-start | bytes 786440 | tf_op jit(solution)/shard_map/ppermute | solution.py:66
  170.4 66.5 %collective-permute-start.7 = (bf16[1024,512]{1,0:T(8,128)(2,1)}, bf16[1024,512]{1,0:T(8,128)(2,1)}, u32[]{:S(2)}, u32[]{:S(2)}) collective-permute-start(bf16[1024,512]{1,0:T(8,128)(2,1)} %dynamic-slice_convert_fusion), channel_id=1, source_target_pairs={{0,1},{1,0},{2,3},{3,2},{4,5},{5,4},{6,7},{7,6},{8,9},{9,8},{10,11... | collective-permute-start | bytes 3145736 | tf_op jit(solution)/shard_map/ppermute | solution.py:66
  173.7 60.9 %collective-permute-start.6 = (bf16[512,512]{1,0:T(8,128)(2,1)}, bf16[512,512]{1,0:T(8,128)(2,1)}, u32[]{:S(2)}, u32[]{:S(2)}) collective-permute-start(bf16[512,512]{1,0:T(8,128)(2,1)} %dynamic-slice_convert_fusion.1), channel_id=1, source_target_pairs={{0,1},{1,0},{2,3},{3,2},{4,5},{5,4},{6,7},{7,6},{8,9},{9,8},{10,11... | collective-permute-start | bytes 1572872 | tf_op jit(solution)/shard_map/ppermute | solution.py:66
  177.1 55.9 %copy-start.34 = (pred[128,16]{1,0:T(32,128)(4,1)S(1)}, pred[128,16]{1,0:T(32,128)(4,1)}, u32[]{:S(2)}) copy-start(pred[128,16]{1,0:T(32,128)(4,1)} %copy-done.33) | copy-start | bytes 6148
  177.1 56.3 %copy-start.31 = (bf16[1024,17]{0,1:T(8,128)(2,1)S(1)}, bf16[1024,17]{0,1:T(8,128)(2,1)}, u32[]{:S(2)}) copy-start(bf16[1024,17]{0,1:T(8,128)(2,1)} %copy-done.30) | copy-start | bytes 104452
  177.1 56.3 %copy-start.40 = (f32[1024,1]{0,1:T(1,128)S(1)}, f32[1024,1]{0,1:T(1,128)}, u32[]{:S(2)}) copy-start(f32[1024,1]{0,1:T(1,128)} %copy-done.39) | copy-start | bytes 12292
  177.1 56.3 %copy-start.48 = (f32[128]{0:T(128)S(1)}, f32[128]{0:T(128)}, u32[]{:S(2)}) copy-start(f32[128]{0:T(128)} %copy-done.47) | copy-start | bytes 1540
  177.1 57.2 %copy-start.18 = (bf16[128,1024]{1,0:T(8,128)(2,1)S(1)}, bf16[128,1024]{1,0:T(8,128)(2,1)}, u32[]{:S(2)}) copy-start(bf16[128,1024]{1,0:T(8,128)(2,1)} %param.23) | copy-start | bytes 786436
  177.1 57.4 %copy-start.21 = (f32[512,1024]{1,0:T(8,128)S(1)}, f32[512,1024]{1,0:T(8,128)}, u32[]{:S(2)}) copy-start(f32[512,1024]{1,0:T(8,128)} %fusion.86) | copy-start | bytes 6291460
  233.7 16.1 %copy-start.43 = (f32[1024]{0:T(1024)}, f32[1024]{0:T(1024)S(1)}, u32[]{:S(2)}) copy-start(f32[1024]{0:T(1024)S(1)} %get-tuple-element.37) | copy-start | bytes 12292
  240.0 7.7 %collective-permute-start.8 = (bf16[128,1024]{1,0:T(8,128)(2,1)S(1)}, bf16[128,1024]{1,0:T(8,128)(2,1)S(1)}, u32[]{:S(2)}, u32[]{:S(2)}) collective-permute-start(bf16[128,1024]{1,0:T(8,128)(2,1)S(1)} %multiply_convert_fusion.4), channel_id=1, source_target_pairs={{0,1},{1,0},{2,3},{3,2},{4,5},{5,4},{6,7},{7,6},{8,9},{9,8},{10,11... | collective-permute-start | bytes 786440 | tf_op jit(solution)/shard_map/ppermute | solution.py:66
  248.2 3.9 %collective-permute-start.9 = (bf16[128,512]{1,0:T(8,128)(2,1)S(1)}, bf16[128,512]{1,0:T(8,128)(2,1)S(1)}, u32[]{:S(2)}, u32[]{:S(2)}) collective-permute-start(bf16[128,512]{1,0:T(8,128)(2,1)S(1)} %get-tuple-element.67), channel_id=1, source_target_pairs={{0,1},{1,0},{2,3},{3,2},{4,5},{5,4},{6,7},{7,6},{8,9},{9,8},{10,11... | collective-permute-start | bytes 393224 | tf_op jit(solution)/shard_map/ppermute | solution.py:66
  250.5 8.8 %collective-permute-start.12 = (f32[512,17]{0,1:T(8,128)}, f32[512,17]{0,1:T(8,128)}, u32[]{:S(2)}, u32[]{:S(2)}) collective-permute-start(f32[512,17]{0,1:T(8,128)} %fusion.52), channel_id=1, source_target_pairs={{0,1},{1,0},{2,3},{3,2},{4,5},{5,4},{6,7},{7,6},{8,9},{9,8},{10,11... | collective-permute-start | bytes 104456 | tf_op jit(solution)/shard_map/ppermute | solution.py:66
  257.8 10.7 %collective-permute-start.10 = (bf16[128,2048]{0,1:T(8,128)(2,1)S(1)}, bf16[128,2048]{0,1:T(8,128)(2,1)S(1)}, u32[]{:S(2)}, u32[]{:S(2)}) collective-permute-start(bf16[128,2048]{0,1:T(8,128)(2,1)S(1)} %pad_maximum_fusion.5), channel_id=1, source_target_pairs={{0,1},{1,0},{2,3},{3,2},{4,5},{5,4},{6,7},{7,6},{8,9},{9,8},{10,11... | collective-permute-start | bytes 1572872 | tf_op jit(solution)/shard_map/ppermute | solution.py:66
  349.2 7.2 %collective-permute-start.11 = (bf16[128,512]{1,0:T(8,128)(2,1)}, bf16[128,512]{1,0:T(8,128)(2,1)}, u32[]{:S(2)}, u32[]{:S(2)}) collective-permute-start(bf16[128,512]{1,0:T(8,128)(2,1)} %get-tuple-element.64), channel_id=1, source_target_pairs={{0,1},{1,0},{2,3},{3,2},{4,5},{5,4},{6,7},{7,6},{8,9},{9,8},{10,11... | collective-permute-start | bytes 393224 | tf_op jit(solution)/shard_map/ppermute | solution.py:66
  (51 other events, 353.8 us)
Sparse Core Ops, SparseCore 0:
  15.6 55.3 all-gather.1
  153.9 95.5 reduce-scatter.1
